TPU v7x, 32 devices: a whole 2x2x4 slice. The times are simulated.
32 devices in a mesh: dp: 8 (over z, x), seq: 4 (over y, core).
Axes of the slice: x: 2, y: 2, z: 4, core: 2. Of those that a mesh axis runs over, the one named last changes fastest.
Arguments:
- tokens: bfloat16 [8, 1024, 1536], P('dp', 'seq'), may hold values from -6 to 6
- modulation: float32 [8, 3, 1536], P('dp'), may hold values from -4 to 4
- heights: int32 [8], P('dp'), may hold values from 16 to 64, as said below
- w_in: bfloat16 [1536, 6144], replicated, may hold values from -0.15625 to 0.15625
- w_x: bfloat16 [3072, 128], replicated, may hold values from -0.109375 to 0.109375
- w_dt: bfloat16 [3072, 96], replicated, may hold values from -0.625 to 0.625
- b_dt: float32 [3072], replicated, may hold values from -7 to -2.5
- a_log: float32 [3072, 16], replicated, may hold values from -1.5 to 1
- d_skip: float32 [3072], replicated, may hold values from 0.5 to 1.5
- conv_w: float32 [3072, 4], replicated, may hold values from -3 to 3
- conv_b: float32 [3072], replicated, may hold values from -0.5 to 0.5
- w_out: bfloat16 [3072, 1536], replicated, may hold values from -0.109375 to 0.109375
- cotangent: bfloat16 [8, 1024, 1536], P('dp', 'seq'), may hold values from -6 to 6
Outputs:
- result: bfloat16 [8, 1024, 1536], P('dp', 'seq')
- grad_tokens: float32 [8, 1024, 1536], P('dp', 'seq')
- grad_w_in: float32 [1536, 6144], P('seq')
- grad_w_x: float32 [3072, 128], P('seq')
- grad_w_dt: float32 [3072, 96], P('seq')
- grad_b_dt: float32 [3072], P('seq')
- grad_a_log: float32 [3072, 16], P('seq')
- grad_d_skip: float32 [3072], P('seq')
- grad_conv_w: float32 [3072, 4], P('seq')
- grad_conv_b: float32 [3072], P('seq')
- grad_w_out: float32 [3072, 1536], P('seq')
Inputs may be any that keep to these rules, and one draw needn't show every extreme that they name: `heights`: each height is 16, 32 or 64; the grid's width is 1024 divided by its height.
All inputs are finite; a program needn't handle non-finite values.
Results may differ from a plain program's by a relative error of at most 0.008.
The roundings to bfloat16 on the way count: a program that leaves them out, or rounds other values in their place, can miss the bound.
Values may be sent and summed in bfloat16 or wider, within the bound.
No kernel may reach another device: no remote copies, remote signals or barrier semaphores. Data moves between devices by JAX's collectives and lax.ppermute only.
A program may use at most 320 MiB of HBM per device.

v0:
```python
import jax
import jax.numpy as jnp
from jax import lax
from jax.sharding import PartitionSpec as P

BLOCK = 16


epsilon = 1e-06
highest = lax.Precision.HIGHEST


def shifted(block, axis, distance):
    devices = range(lax.axis_size(axis))
    route = [(i - distance, i) for i in devices if i - distance in devices]
    return lax.ppermute(block, axis, route)


def carried_in(array, axis, combine, identity, reverse):
    devices, index = (lax.axis_size(axis), lax.axis_index(axis))
    everything = jax.tree.map(
        lambda part, kind: lax.all_gather(part.astype(kind), axis),
        array,
        (jnp.bfloat16, jnp.bfloat16),
    )
    start = jax.tree.map(
        lambda part, zero: jnp.broadcast_to(jnp.asarray(zero, part.dtype), part.shape),
        array,
        identity,
    )

    def lap(k, before):
        at = devices - 1 - k if reverse else k
        reached = at > index if reverse else at < index
        new = combine(
            before, jax.tree.map(lambda part, own: part[at].astype(own.dtype), everything, array)
        )
        return jax.tree.map(lambda a, b: jnp.where(reached, a, b), new, before)

    return lax.fori_loop(0, devices, lap, start)


def silu_slope(value):
    sigmoid = jax.nn.sigmoid(value)
    return sigmoid * (1.0 + value * (1.0 - sigmoid))


def normalize(rows_in, shift, scale):
    mean = jnp.mean(rows_in, axis=-1, keepdims=True)
    centered = rows_in - mean
    variance = jnp.mean(centered * centered, axis=-1, keepdims=True)
    return centered * lax.rsqrt(variance + epsilon) * (1.0 + scale) + shift


def chain(earlier, later):
    return (earlier[0] * later[0], later[0] * earlier[1] + later[1])


def blocks_first(value, block):
    shaped = value.reshape((value.shape[0], value.shape[1] // block, block) + value.shape[2:])
    return jnp.moveaxis(shaped, 1, 0)


def tokens_back(value):
    moved = jnp.moveaxis(value, 0, 1)
    return moved.reshape((moved.shape[0], moved.shape[1] * moved.shape[2]) + moved.shape[3:])


def scan_local(delta, b_mat, c_mat, inputs, a_state, start):

    def step_block(carried, pieces):
        d_part, b_part, c_part, v_part = pieces
        outputs = []
        for position in range(BLOCK):
            decay = jnp.exp(d_part[:, position, None, :] * a_state)
            carried = (
                decay * carried
                + (d_part[:, position] * v_part[:, position])[:, None, :]
                * b_part[:, position, :, None]
            )
            outputs.append(jnp.sum(carried * c_part[:, position, :, None], axis=1))
        return (carried, jnp.stack(outputs, axis=1))

    pieces = (
        blocks_first(delta, BLOCK),
        blocks_first(b_mat, BLOCK),
        blocks_first(c_mat, BLOCK),
        blocks_first(inputs, BLOCK),
    )
    final, outputs = lax.scan(jax.checkpoint(step_block), start, pieces)
    return (tokens_back(outputs), final)


def carry_terms(cumul, c_mat, a_state, start):

    def one_block(pieces):
        cum_part, c_part = pieces
        weight = jnp.exp(cum_part[:, :, None, :] * a_state) * start[:, None]
        return jnp.einsum("ibne,ibn->ibe", weight, c_part, precision=highest)

    return tokens_back(lax.map(one_block, (blocks_first(cumul, BLOCK), blocks_first(c_mat, BLOCK))))


def carry_grad(cumul, c_mat, a_state, grads):

    def one_block(total, pieces):
        cum_part, c_part, g_part = pieces
        weight = jnp.exp(cum_part[:, :, None, :] * a_state)
        return (
            total + jnp.einsum("ibne,ibe,ibn->ine", weight, g_part, c_part, precision=highest),
            None,
        )

    start = jnp.zeros((cumul.shape[0],) + a_state.shape, jnp.float32)
    total, _ = lax.scan(
        one_block,
        start,
        (blocks_first(cumul, BLOCK), blocks_first(c_mat, BLOCK), blocks_first(grads, BLOCK)),
    )
    return total


def layout_maps(heights, seq_len, parts):
    total = seq_len * parts
    tall = heights[:, None]
    wide = total // tall
    h_part = tall // parts
    w_part = wide // parts
    block_len = seq_len // parts
    position = jnp.arange(seq_len, dtype=jnp.int32)[None, :]
    target = position // block_len
    remain = position % block_len
    col_in = remain // h_part
    row_in = remain % h_part
    send_take = row_in * wide + target * w_part + col_in
    col_q = position // tall
    row_q = position % tall
    recv_take = row_q // h_part * block_len + col_q * h_part + row_q % h_part
    recv_back = col_in * tall + target * h_part + row_in
    row_l = position // wide
    col_l = position % wide
    send_back = col_l // w_part * block_len + col_l % w_part * h_part + row_l
    return (send_take, recv_take, recv_back, send_back)


def pick(values, index):
    return jnp.take_along_axis(values, index[:, :, None], axis=1)


def contract_rows(left, right):
    return lax.dot_general(
        left, right, (((0,), (0,)), ((), ())), preferred_element_type=jnp.float32
    )


def contract_cols(left, right):
    return lax.dot_general(
        left, right, (((1,), (1,)), ((), ())), preferred_element_type=jnp.float32
    )


def delta_pre(proj, w_dt, b_dt, low_rank):
    return (
        lax.dot_general(
            proj[..., :low_rank], w_dt, (((2,), (1,)), ((), ())), preferred_element_type=jnp.float32
        )
        + b_dt
    )


def delta_back(d_delta, pre_delta, proj, w_dt, low_rank):
    d_pre = d_delta * jax.nn.sigmoid(pre_delta)
    grad_weight = jnp.einsum(
        "ise,isr->er", d_pre, proj[..., :low_rank].astype(jnp.float32), precision=highest
    )
    grad_bias = jnp.sum(d_pre, axis=(0, 1))
    d_low = jnp.einsum("ise,er->isr", d_pre, w_dt.astype(jnp.float32), precision=highest)
    return (grad_weight, grad_bias, d_low)


def shuffle_columns(matrix, parts, data_parts):
    count = matrix.shape[0]
    return matrix.reshape(count, parts, data_parts, -1).swapaxes(1, 2).reshape(matrix.shape)


def shuffle_rows(values, parts, data_parts):
    shaped = values.reshape(
        (parts, data_parts, values.shape[0] // (parts * data_parts)) + values.shape[1:]
    )
    return shaped.swapaxes(0, 1).reshape(values.shape)


def shards(
    tokens,
    modulation,
    heights,
    w_in,
    w_x,
    w_dt,
    b_dt,
    a_log,
    d_skip,
    conv_w,
    conv_b,
    w_out,
    cotangent,
):
    item_count, seq_len, model_width = tokens.shape
    parts = lax.axis_size("seq")
    inner_width = w_out.shape[0]
    low_rank = w_dt.shape[1]
    state_size = a_log.shape[1]
    conv_taps = conv_w.shape[1]
    row_count = item_count * seq_len
    a_state = -jnp.exp(a_log.T)
    shift = modulation[:, 0:1]
    scale = modulation[:, 1:2]
    gate = modulation[:, 2:3]
    zero_state = jnp.zeros((item_count, state_size, inner_width), jnp.float32)
    identity = (jnp.ones((item_count, state_size, inner_width), jnp.float32), zero_state)
    x_full = tokens.astype(jnp.float32)
    normed, norm_back = jax.vjp(lambda rows_in: normalize(rows_in, shift, scale), x_full)
    h_low = normed.astype(jnp.bfloat16).reshape(row_count, model_width)
    xz = jnp.dot(h_low, w_in, preferred_element_type=jnp.float32)
    x_conv = xz[:, :inner_width].astype(jnp.bfloat16).reshape(item_count, seq_len, inner_width)
    z_gate = xz[:, inner_width:].reshape(item_count, seq_len, inner_width)
    rim = shifted(x_conv[:, seq_len - conv_taps + 1 :], "seq", 1)
    padded = jnp.concatenate([rim, x_conv], axis=1).astype(jnp.float32)
    pre_conv = conv_b + sum(
        (padded[:, offset : offset + seq_len] * conv_w[:, offset] for offset in range(conv_taps))
    )
    u_low = jax.nn.silu(pre_conv).astype(jnp.bfloat16)
    u_full = u_low.astype(jnp.float32)
    proj = jnp.dot(u_low.reshape(row_count, inner_width), w_x, preferred_element_type=jnp.float32)
    proj = proj.astype(jnp.bfloat16).reshape(item_count, seq_len, -1)
    pre_row = delta_pre(proj, w_dt, b_dt, low_rank)
    delta_row = jax.nn.softplus(pre_row)
    b_row = proj[..., low_rank : low_rank + state_size].astype(jnp.float32)
    c_row = proj[..., low_rank + state_size :].astype(jnp.float32)
    cum_row = jnp.cumsum(delta_row, axis=1)
    zero_row, end_row = scan_local(delta_row, b_row, c_row, u_full, a_state, zero_state)
    decay_row = jnp.exp(cum_row[:, -1, None, :] * a_state)
    start_row = carried_in((decay_row, end_row), "seq", chain, identity, False)[1]
    y_fwd = zero_row + carry_terms(cum_row, c_row, a_state, start_row)
    send_take, recv_take, recv_back, send_back = layout_maps(heights, seq_len, parts)
    recv_rev = recv_take[:, ::-1]
    back_index = seq_len - 1 - recv_back
    col_u, col_proj = (
        lax.all_to_all(pick(u_low, send_take), "seq", split_axis=1, concat_axis=1, tiled=True),
        lax.all_to_all(pick(proj, send_take), "seq", split_axis=1, concat_axis=1, tiled=True),
    )
    col_u = pick(col_u, recv_rev).astype(jnp.float32)
    col_proj = pick(col_proj, recv_rev)
    pre_col = delta_pre(col_proj, w_dt, b_dt, low_rank)
    delta_col = jax.nn.softplus(pre_col)
    b_col = col_proj[..., low_rank : low_rank + state_size].astype(jnp.float32)
    c_col = col_proj[..., low_rank + state_size :].astype(jnp.float32)
    cum_col = jnp.cumsum(delta_col, axis=1)
    zero_col, end_col = scan_local(delta_col, b_col, c_col, col_u, a_state, zero_state)
    decay_col = jnp.exp(cum_col[:, -1, None, :] * a_state)
    start_col = carried_in((decay_col, end_col), "seq", chain, identity, True)[1]
    y_col = (zero_col + carry_terms(cum_col, c_col, a_state, start_col)).astype(jnp.bfloat16)
    returned = lax.all_to_all(
        pick(y_col, back_index), "seq", split_axis=1, concat_axis=1, tiled=True
    )
    y_bwd = pick(returned, send_back).astype(jnp.float32)
    y_all = y_fwd + y_bwd + d_skip * u_full
    silu_z = jax.nn.silu(z_gate)
    gated = (y_all * silu_z).astype(jnp.bfloat16).reshape(row_count, inner_width)
    branch = jnp.dot(gated, w_out, preferred_element_type=jnp.float32).reshape(
        item_count, seq_len, model_width
    )
    result = (x_full + gate * branch).astype(jnp.bfloat16)
    d_res = cotangent.astype(jnp.float32)
    d_branch = (gate * d_res).astype(jnp.bfloat16).reshape(row_count, model_width)
    d_gated = contract_cols(d_branch, w_out).reshape(item_count, seq_len, inner_width)
    d_y = d_gated * silu_z
    d_z = d_gated * y_all * silu_slope(z_gate)
    g_dskip = jnp.sum(d_y * u_full, axis=(0, 1))
    col_dy = lax.all_to_all(
        pick(d_y.astype(jnp.bfloat16), send_take), "seq", split_axis=1, concat_axis=1, tiled=True
    )
    col_dy = pick(col_dy, recv_rev).astype(jnp.float32)
    g_col = carry_grad(cum_col, c_col, a_state, col_dy)
    lam_col = carried_in((decay_col, g_col), "seq", chain, identity, False)[1]
    _, col_pull = jax.vjp(
        lambda d_in, b_in, c_in, v_in, a_in: scan_local(d_in, b_in, c_in, v_in, a_in, start_col),
        delta_col,
        b_col,
        c_col,
        col_u,
        a_state,
    )
    dd_col, db_col, dc_col, du_col, da_col = col_pull((col_dy, lam_col))
    gw_col, gb_col, dlow_col = delta_back(dd_col, pre_col, col_proj, w_dt, low_rank)
    dproj_col = jnp.concatenate([dlow_col, db_col, dc_col], axis=2).astype(jnp.bfloat16)
    back_u, back_proj = (
        lax.all_to_all(
            pick(du_col.astype(jnp.bfloat16), back_index),
            "seq",
            split_axis=1,
            concat_axis=1,
            tiled=True,
        ),
        lax.all_to_all(pick(dproj_col, back_index), "seq", split_axis=1, concat_axis=1, tiled=True),
    )
    back_u = pick(back_u, send_back).astype(jnp.float32)
    back_proj = pick(back_proj, send_back).astype(jnp.float32)
    g_row = carry_grad(cum_row, c_row, a_state, d_y)
    lam_row = carried_in((decay_row, g_row), "seq", chain, identity, True)[1]
    _, row_pull = jax.vjp(
        lambda d_in, b_in, c_in, v_in, a_in: scan_local(d_in, b_in, c_in, v_in, a_in, start_row),
        delta_row,
        b_row,
        c_row,
        u_full,
        a_state,
    )
    dd_row, db_row, dc_row, du_row, da_row = row_pull((d_y, lam_row))
    gw_row, gb_row, dlow_row = delta_back(dd_row, pre_row, proj, w_dt, low_rank)
    g_wdt = gw_row + gw_col
    g_bdt = gb_row + gb_col
    g_alog = ((da_row + da_col) * a_state).T
    d_proj = (jnp.concatenate([dlow_row, db_row, dc_row], axis=2) + back_proj).astype(jnp.bfloat16)
    d_proj = d_proj.reshape(row_count, -1)
    g_wx = contract_rows(u_low.reshape(row_count, inner_width), d_proj)
    d_u = (
        du_row
        + back_u
        + d_y * d_skip
        + contract_cols(d_proj, w_x).reshape(item_count, seq_len, inner_width)
    )
    d_pre_conv = d_u * silu_slope(pre_conv)
    g_convb = jnp.sum(d_pre_conv, axis=(0, 1))
    g_convw = jnp.stack(
        [
            jnp.sum(padded[:, offset : offset + seq_len] * d_pre_conv, axis=(0, 1))
            for offset in range(conv_taps)
        ],
        axis=1,
    )
    d_padded = jnp.zeros((item_count, seq_len + conv_taps - 1, inner_width), jnp.float32)
    for offset in range(conv_taps):
        d_padded = d_padded.at[:, offset : offset + seq_len].add(conv_w[:, offset] * d_pre_conv)
    rim_back = shifted(d_padded[:, : conv_taps - 1].astype(jnp.bfloat16), "seq", -1).astype(
        jnp.float32
    )
    d_xconv = d_padded[:, conv_taps - 1 :].at[:, seq_len - conv_taps + 1 :].add(rim_back)
    d_xz = (
        jnp.concatenate([d_xconv, d_z], axis=2)
        .astype(jnp.bfloat16)
        .reshape(row_count, 2 * inner_width)
    )
    d_h = contract_cols(d_xz, w_in).reshape(item_count, seq_len, model_width)
    d_x = d_res + norm_back(d_h)[0]
    data_parts = lax.axis_size("dp")
    g_win = contract_rows(shuffle_columns(h_low, parts, data_parts), d_xz)
    g_out = contract_rows(shuffle_columns(gated, parts, data_parts), d_branch)
    summed = (
        lax.psum_scatter(g_win, ("dp", "seq"), scatter_dimension=0, tiled=True),
        lax.psum_scatter(g_out, ("dp", "seq"), scatter_dimension=0, tiled=True),
        lax.psum_scatter(
            shuffle_rows(g_wx, parts, data_parts), ("dp", "seq"), scatter_dimension=0, tiled=True
        ),
        lax.psum_scatter(
            shuffle_rows(g_wdt, parts, data_parts), ("dp", "seq"), scatter_dimension=0, tiled=True
        ),
        lax.psum_scatter(
            shuffle_rows(g_bdt, parts, data_parts), ("dp", "seq"), scatter_dimension=0, tiled=True
        ),
        lax.psum_scatter(
            shuffle_rows(g_alog, parts, data_parts), ("dp", "seq"), scatter_dimension=0, tiled=True
        ),
        lax.psum_scatter(
            shuffle_rows(g_dskip, parts, data_parts), ("dp", "seq"), scatter_dimension=0, tiled=True
        ),
        lax.psum_scatter(
            shuffle_rows(g_convw, parts, data_parts), ("dp", "seq"), scatter_dimension=0, tiled=True
        ),
        lax.psum_scatter(
            shuffle_rows(g_convb, parts, data_parts), ("dp", "seq"), scatter_dimension=0, tiled=True
        ),
    )
    final = (
        lax.all_gather(summed[0].astype(jnp.bfloat16), "dp", axis=0, tiled=True).astype(
            jnp.float32
        ),
        lax.all_gather(summed[1].astype(jnp.bfloat16), "dp", axis=0, tiled=True).astype(
            jnp.float32
        ),
        lax.all_gather(summed[2].astype(jnp.bfloat16), "dp", axis=0, tiled=True).astype(
            jnp.float32
        ),
        lax.all_gather(summed[3].astype(jnp.bfloat16), "dp", axis=0, tiled=True).astype(
            jnp.float32
        ),
        lax.all_gather(summed[4].astype(jnp.bfloat16), "dp", axis=0, tiled=True).astype(
            jnp.float32
        ),
        lax.all_gather(summed[5].astype(jnp.bfloat16), "dp", axis=0, tiled=True).astype(
            jnp.float32
        ),
        lax.all_gather(summed[6].astype(jnp.bfloat16), "dp", axis=0, tiled=True).astype(
            jnp.float32
        ),
        lax.all_gather(summed[7].astype(jnp.bfloat16), "dp", axis=0, tiled=True).astype(
            jnp.float32
        ),
        lax.all_gather(summed[8].astype(jnp.bfloat16), "dp", axis=0, tiled=True).astype(
            jnp.float32
        ),
    )
    return (
        result,
        d_x,
        final[0],
        final[2],
        final[3],
        final[4],
        final[5],
        final[6],
        final[7],
        final[8],
        final[1],
    )


def solution(mesh):
    placed = (
        P("dp", "seq", None),
        P("dp", None, None),
        P("dp"),
        P(),
        P(),
        P(),
        P(),
        P(),
        P(),
        P(),
        P(),
        P(),
        P("dp", "seq", None),
    )
    return jax.shard_map(
        shards,
        mesh=mesh,
        in_specs=placed,
        out_specs=(
            P("dp", "seq", None),
            P("dp", "seq", None),
            P("seq", None),
            P("seq", None),
            P("seq", None),
            P("seq"),
            P("seq", None),
            P("seq"),
            P("seq", None),
            P("seq"),
            P("seq", None),
        ),
        check_vma=False,
    )
```

profile of v0, /device:TPU:0, one launch (start us, length us, event | category | flops | bytes accessed | tf_op | source)
XLA Modules:
  0.0 2948.5 jit_solution(13221621784947398139)
XLA Ops:
  12.5 9.6 fusion.245
  37.6 15.6 fusion.218
  54.0 4.6 compare_select_fusion.1
  58.6 6.0 fusion.223
  64.6 4.6 copy.350
  76.8 262.7 %while.213 = (s32[]{:T(128)}, f32[1,16,3072]{2,1,0:T(8,128)S(1)}, f32[16,1,16,3072]{3,2,1,0:T(8,128)}, f32[16,1,16,3072]{3,2,1,0:T(8,128)}, f32[16,3072]{1,0:T(8...) while((s32[]{:T(128)}, f32[1,16,3072]{2,1,0:T(8,128)S(1)}, ...), condition=%wide.region_19.20_spmd.clone, body=%wide.region_2.19_spmd.clone.sunk | while | flops 7176195 | bytes 6304952 | solution.py:90
  349.7 7.9 all-gather.1
  361.0 6.0 gather_fusion.6
  373.8 90.6 %while.217 = (s32[]{:T(128)}, f32[1,16,3072]{2,1,0:T(8,128)S(1)}, f32[16,1,16,16]{3,2,1,0:T(8,128)}, f32[16,1,16,3072]{3,2,1,0:T(8,128)}, f32[16,3072]{1,0:T(8,1...) while((s32[]{:T(128)}, f32[1,16,3072]{2,1,0:T(8,128)S(1)}, ...), condition=%wide.region_51.56_spmd.clone, body=%wide.region_50.55_spmd.clone.sunk | while | flops 11108355 | bytes 8459375 | solution.py:115
  467.3 7.5 all-gather.4
  479.8 11.3 reduce.959
  493.7 5.5 copy.493
  499.1 11.3 reduce.960
  518.8 5.9 compare_select_fusion
  524.7 6.0 fusion.221
  530.7 4.5 copy.363
  540.7 7.4 all-gather
  554.6 73.4 %while.211 = (s32[]{:T(128)}, f32[1,16,3072]{2,1,0:T(8,128)S(1)}, f32[16,1,16,3072]{3,2,1,0:T(8,128)}, f32[16,1,16,3072]{3,2,1,0:T(8,128)}, f32[1,16,3072]{2,1,0...) while((s32[]{:T(128)}, f32[1,16,3072]{2,1,0:T(8,128)S(1)}, ...), condition=%wide.region_55.60_spmd, body=%wide.region_54.59_spmd.sunk | while | flops 3194882 | bytes 3138665 | solution.py:90
  634.5 74.0 %while.209 = (s32[]{:T(128)}, f32[16,1,16,3072]{3,2,1,0:T(8,128)}, f32[16,1,16,3072]{3,2,1,0:T(8,128)}, f32[16,3072]{1,0:T(8,128)S(1)}, f32[1,16,3072]{2,1,0:T(8,128)S(1)}, /*index=5*/f32[16,1,16,16]{3,2,1,0:T(8,128)}, s32[]{:T(128)}) while((s32[]{:T(128)}, f32[16,1,16,3072]{3,2,1,0:T(8,128)}, f32[16,1,16,3072]{3,2,1,0:T(8,128)}, ...), condition=%wide.region_25.26_spmd, body=%wide.region_24.25_spmd.sunk | while | flops 11010050 | bytes 1576033 | solution.py:101
  709.9 7.6 all-gather.2
  739.3 90.5 %while.220 = (s32[]{:T(128)}, f32[1,16,3072]{2,1,0:T(8,128)S(1)}, f32[16,1,16,16]{3,2,1,0:T(8,128)}, f32[16,1,16,3072]{3,2,1,0:T(8,128)}, f32[16,3072]{1,0:T(8,1...) while((s32[]{:T(128)}, f32[1,16,3072]{2,1,0:T(8,128)S(1)}, ...), condition=%wide.region_123.128_spmd.clone, body=%wide.region_122.127_spmd.clone.sunk | while | flops 11108355 | bytes 8459375 | solution.py:115
  829.9 7.0 all-gather.5
  845.4 86.0 %while.215 = (s32[]{:T(128)}, f32[1,16,3072]{2,1,0:T(8,128)S(1)}, f32[16,1,16,3072]{3,2,1,0:T(8,128)}, f32[16,1,16,3072]{3,2,1,0:T(8,128)}, f32[16,3072]{1,0:T(8...) while((s32[]{:T(128)}, f32[1,16,3072]{2,1,0:T(8,128)S(1)}, ...), condition=%wide.region_43.48_spmd.clone, body=%wide.region_26.47_spmd.clone.sunk | while | flops 7176195 | bytes 6155140 | solution.py:90
  931.5 7.0 all-gather.3
  944.8 58.6 %while.212 = (s32[]{:T(128)}, f32[1,16,3072]{2,1,0:T(8,128)S(1)}, f32[16,1,16,3072]{3,2,1,0:T(8,128)}, f32[16,1,16,3072]{3,2,1,0:T(8,128)}, f32[1,16,3072]{2,1,0...) while((s32[]{:T(128)}, f32[1,16,3072]{2,1,0:T(8,128)S(1)}, ...), condition=%wide.region_127.132_spmd, body=%wide.region_126.131_spmd.sunk | while | flops 3194882 | bytes 3138665 | solution.py:90
  1005.5 355.2 %while.222 = (s32[]{:T(128)}, f32[16,3072]{1,0:T(8,128)}, f32[1,16,3072]{2,1,0:T(8,128)S(1)}, f32[16,1,16,3072]{3,2,1,0:T(8,128)}, bf16[16,1,16,16]{3,2,1,0:T(8,...) while((s32[]{:T(128)}, f32[16,3072]{1,0:T(8,128)}, ...), condition=%wide.region_193.198_spmd.clone, body=%wide.region_128.197_spmd.clone.sunk | while | flops 27335684 | bytes 20248216 | solution.py:90
  1362.9 74.2 %while.210 = (s32[]{:T(128)}, f32[16,1,16,3072]{3,2,1,0:T(8,128)}, f32[16,1,16,3072]{3,2,1,0:T(8,128)}, f32[16,3072]{1,0:T(8,128)S(1)}, f32[1,16,3072]{2,1,0:T(8,128)S(1)}, /*index=5*/f32[16,1,16,16]{3,2,1,0:T(8,128)}, s32[]{:T(128)}) while((s32[]{:T(128)}, f32[16,1,16,3072]{3,2,1,0:T(8,128)}, f32[16,1,16,3072]{3,2,1,0:T(8,128)}, ...), condition=%wide.region_49.54_spmd, body=%wide.region_48.53_spmd.sunk | while | flops 11010050 | bytes 1576033 | solution.py:101
  1453.2 11.5 reduce.961
  1470.8 4.5 while.218
  1475.3 5.0 add.1340
  1480.3 10.5 all-to-all-done.2
  1497.2 6.2 gather_fusion.5
  1503.4 6.3 fusion.242
  1513.9 8.2 fusion.247
  1527.4 366.7 %while.219 = (s32[]{:T(128)}, f32[16,3072]{1,0:T(8,128)}, f32[1,16,3072]{2,1,0:T(8,128)S(1)}, f32[16,1,16,3072]{3,2,1,0:T(8,128)}, f32[16,1,16,16]{3,2,1,0:T(8,1...) while((s32[]{:T(128)}, f32[16,3072]{1,0:T(8,128)}, ...), condition=%wide.region_121.126_spmd.clone, body=%wide.region_56.125_spmd.clone.sunk | while | flops 27335684 | bytes 20248216 | solution.py:90
  1895.9 7.3 fusion.305
  1913.0 5.5 copy.490
  1918.5 12.4 reduce.963
  1935.3 4.5 all-to-all-start.4
  1947.2 12.7 all-to-all-done.4
  1967.9 5.9 gather_fusion.9
  1973.9 5.2 broadcast_multiply_fusion
  1984.1 8.5 scatter-add.15
  1992.6 5.4 slice_add_fusion.1
  1998.0 8.5 scatter-add.16
  2008.8 9.9 multiply_reduce_fusion.129
  2025.3 14.8 fusion.233
  2049.6 5.4 convolution_add_fusion.2
  2069.3 321.1 %reduce-scatter.13.cloned.1.call-done = f32[48,6144]{1,0:T(8,128)} async-done(((f32[1536,6144]{1,0:T(8,128)}), f32[48,6144]{1,0:T(8,128)}) %reduce-scatter.13.cloned.1.call-update) | async-done | bytes 1179664 | tf_op jit(solution)/shard_map/reduce_scatter | solution.py:360
  2394.3 98.5 %reduce-scatter.21.cloned.1.call-done = f32[96,16]{1,0:T(8,128)} async-done(((f32[3072,16]{1,0:T(8,128)}), f32[96,16]{1,0:T(8,128)}) %reduce-scatter.21.cloned.1.call-update) | async-done | bytes 6160
  2493.6 30.4 %all-gather.6 = bf16[8,96,16]{1,2,0:T(8,128)(2,1)S(1)} all-gather(bf16[1,96,16]{1,2,0:T(8,128)(2,1)S(1)} %bitcast.4516), channel_id=1, replica_groups=mesh['dp'=8,'seq'=4] {'dp'}, dimensions={0}, use_global_device_ids=true | all-gather | bytes 27648 | tf_op jit(solution)/shard_map/all_gather | solution.py:400
  2524.9 38.5 %all-reduce.167 = (bf16[3072]{0:T(1024)(128)(2,1)S(1)}, bf16[3072]{0:T(1024)(128)(2,1)S(1)}, bf16[3072]{0:T(1024)(128)(2,1)S(1)}) all-reduce(f32[3072]{0:T(1024)S(1)} %reshape.15453, f32[3072]{0:T(1024)S(1)} %reshape.15457, f32[3072]{0:T(1024)S(1)} %reshape.15460), channel_id=11, replica_groups=mesh['dp'=8,'seq'=4] {'dp','seq'}, use_global_device_ids=true, to_apply=%region_201.206.clone | all-reduce | flops 9216 | bytes 55296
  2564.2 20.9 all-reduce.168
  2587.0 7.4 fusion.228
  2594.4 10.0 fusion.239
  2607.6 16.3 all-gather.7
  2624.5 72.3 %reduce-scatter.19.cloned.1.call-done = f32[96,96]{1,0:T(8,128)} async-done(((f32[3072,96]{1,0:T(8,128)}), f32[96,96]{1,0:T(8,128)}) %reduce-scatter.19.cloned.1.call-update) | async-done | bytes 36880
  2697.9 30.6 %all_gather.81 = bf16[768,96]{1,0:T(8,128)(2,1)S(1)} all-gather(bf16[96,96]{1,0:T(8,128)(2,1)S(1)} %copy.410), channel_id=1, replica_groups=mesh['dp'=8,'seq'=4] {'dp'}, dimensions={0}, use_global_device_ids=true | all-gather | bytes 165888 | tf_op jit(solution)/shard_map/all_gather | solution.py:394
  2729.4 70.1 %reduce-scatter.15.cloned.1.call-done = f32[96,128]{1,0:T(8,128)} async-done(((f32[3072,128]{1,0:T(8,128)}), f32[96,128]{1,0:T(8,128)}) %reduce-scatter.15.cloned.1.call-update) | async-done | bytes 49168 | tf_op jit(solution)/shard_map/reduce_scatter | solution.py:362
  2800.3 30.9 %all_gather.80 = bf16[768,128]{1,0:T(8,128)(2,1)S(1)} all-gather(bf16[96,128]{1,0:T(8,128)(2,1)S(1)} %convert_element_type.373), channel_id=1, replica_groups=mesh['dp'=8,'seq'=4] {'dp'}, dimensions={0}, use_global_device_ids=true | all-gather | bytes 221184 | tf_op jit(solution)/shard_map/all_gather | solution.py:391
  2832.0 21.3 all-gather.13.cloned.1.call-done
  2853.3 4.5 convert_element_type.388
  2857.8 76.4 %all-gather.11.cloned.1.call-done = bf16[384,6144]{1,0:T(8,128)(2,1)} async-done(((bf16[48,6144]{1,0:T(8,128)(2,1)}), bf16[384,6144]{1,0:T(8,128)(2,1)}) %all-gather.11.cloned.1.call-update) | async-done | bytes 4718608 | tf_op jit(solution)/shard_map/all_gather | solution.py:385
  2934.2 7.2 convert_element_type.372
  (3702 shorter events, 1772.3 us)
Async XLA Ops:
  7.2 46.1 %copy-start = (bf16[3072,128]{1,0:T(8,128)(2,1)S(1)}, bf16[3072,128]{1,0:T(8,128)(2,1)}, u32[]{:S(2)}) copy-start(bf16[3072,128]{1,0:T(8,128)(2,1)} %param.63) | copy-start | bytes 2359300
  8.1 29.5 %copy-start.109 = (f32[1536]{0:T(1024)}, f32[1536]{0:T(1024)S(1)}, u32[]{:S(2)}) copy-start(f32[1536]{0:T(1024)S(1)} %get-tuple-element.2617) | copy-start | bytes 18436
  12.5 9.6 copy-start.54
  25.0 12.1 collective-permute-start
  30.9 22.3 copy-start.95
  30.9 22.3 copy-start.97
  31.0 22.3 copy-start.99
  31.0 22.3 copy-start.125
  37.6 15.6 copy-start.5
  37.6 16.3 copy-start.65
  37.6 16.3 copy-start.138
  53.2 313.7 %copy-start.1 = (bf16[1,256,3072]{2,1,0:T(8,128)(2,1)}, bf16[1,256,3072]{2,1,0:T(8,128)(2,1)S(1)}, u32[]{:S(2)}) copy-start(bf16[1,256,3072]{2,1,0:T(8,128)(2,1)S(1)} %get-tuple-element.2864) | copy-start | bytes 4718596
  53.9 16.6 copy-start.73
  342.7 18.3 copy-start.121
  345.8 167.5 %all-to-all-start = ((bf16[4,2,4096]{2,1,0:T(2,128)(2,1)}), bf16[4,2,4096]{2,1,0:T(2,128)(2,1)}, u32[]{:S(2)}, u32[]{:S(2)}) async-start(bf16[4,2,4096]{2,1,0:T(2,128)(2,1)} %reshape.15797), calls=%async_computation | async-start | bytes 131072 | tf_op jit(solution)/shard_map/all_to_all | solution.py:250
  373.7 90.7 %copy-start.43 = (bf16[256,3072]{1,0:T(8,128)(2,1)S(1)}, bf16[256,3072]{1,0:T(8,128)(2,1)}, u32[]{:S(2)}) copy-start(bf16[256,3072]{1,0:T(8,128)(2,1)} %gather_fusion.6) | copy-start | bytes 4718596
  373.7 90.7 %copy-start.132 = (pred[256]{0:T(512)(128)(4,1)S(1)}, pred[256]{0:T(512)(128)(4,1)}, u32[]{:S(2)}) copy-start(pred[256]{0:T(512)(128)(4,1)} %get-tuple-element.2874) | copy-start | bytes 772
  513.3 114.7 %all-to-all-start.3 = ((bf16[4,2,98304]{2,1,0:T(2,128)(2,1)}), bf16[4,2,98304]{2,1,0:T(2,128)(2,1)S(1)}, u32[]{:S(2)}, u32[]{:S(2)}) async-start(bf16[4,2,98304]{2,1,0:T(2,128)(2,1)} %reshape.15799), calls=%async_computation.3 | async-start | bytes 3145728 | tf_op jit(solution)/shard_map/all_to_all | solution.py:280
  536.0 12.1 copy-start.36
  628.0 97.4 %all-to-all-start.1 = ((bf16[4,2,98304]{2,1,0:T(2,128)(2,1)}), bf16[4,2,98304]{2,1,0:T(2,128)(2,1)}, u32[]{:S(2)}, u32[]{:S(2)}) async-start(bf16[4,2,98304]{2,1,0:T(2,128)(2,1)} %reshape.15801), calls=%async_computation.1 | async-start | bytes 3145728 | tf_op jit(solution)/shard_map/all_to_all | solution.py:249
  634.4 74.0 %copy-start.71 = (bf16[1,256,128]{2,1,0:T(8,128)(2,1)S(1)}, bf16[1,256,128]{2,1,0:T(8,128)(2,1)}, u32[]{:S(2)}) copy-start(bf16[1,256,128]{2,1,0:T(8,128)(2,1)} %copy-done.70) | copy-start | bytes 196612
  634.5 75.4 %copy-start.78 = (bf16[16,3072]{1,0:T(8,128)(2,1)S(1)}, bf16[16,3072]{1,0:T(8,128)(2,1)}, u32[]{:S(2)}) copy-start(bf16[16,3072]{1,0:T(8,128)(2,1)} %get-tuple-element.3357) | copy-start | bytes 294916
  1011.3 9.5 copy-start.21
  1122.3 9.5 copy-start.21
  1144.5 9.5 copy-start.21
  1166.7 9.5 copy-start.21
  1188.9 9.5 copy-start.21
  1362.9 74.2 %copy-start.119 = (s32[1024]{0:T(1024)S(1)}, s32[1024]{0:T(1024)}, u32[]{:S(2)}) copy-start(s32[1024]{0:T(1024)} %pad_clamp_fusion.1) | copy-start | bytes 12292
  1467.2 23.6 all-to-all-start.2
  1470.8 596.2 %reduce-scatter.17.cloned.1.call-start = ((), (), s32[]{:S(2)}) async-start(), calls=%async_computation.15 | async-start | bytes 19464192 | tf_op jit(solution)/shard_map/reduce_scatter | solution.py:361
  1533.7 9.5 copy-start.22
  1533.7 9.5 copy-start.25
  1533.7 9.5 copy-start.26
  1556.7 9.5 copy-start.22
  1556.7 9.5 copy-start.25
  1556.7 9.5 copy-start.26
  1602.5 9.5 copy-start.22
  1625.4 9.5 copy-start.22
  1717.1 9.5 copy-start.22
  1909.5 25.7 all-to-all-start.5
  1935.3 24.7 all-to-all-start.4
  1939.8 450.6 %reduce-scatter.13.cloned.1.call-start = ((), (), s32[]{:S(2)}) async-start(), calls=%async_computation.12 | async-start | bytes 38928384 | tf_op jit(solution)/shard_map/reduce_scatter | solution.py:360
  1942.4 31.5 %copy-start.88 = (f32[1,256,16]{1,2,0:T(8,128)}, f32[1,256,16]{1,2,0:T(8,128)S(1)}, u32[]{:S(2)}) copy-start(f32[1,256,16]{1,2,0:T(8,128)S(1)} %copy.432) | copy-start | bytes 49156
  1946.2 27.7 copy-start.79
  1947.2 26.6 copy-start.81
  1998.0 10.7 copy-start.96
  2007.5 11.2 collective-permute-start.1
  2040.1 452.6 %reduce-scatter.21.cloned.1.call-start = ((), (), s32[]{:S(2)}) async-start(), calls=%async_computation.18 | async-start | bytes 1622016
  2043.2 563.5 %reduce-scatter.23.cloned.1.call-start = ((), (), s32[]{:S(2)}) async-start(), calls=%async_computation.19 | async-start | bytes 1622016
  2049.5 647.4 %reduce-scatter.19.cloned.1.call-start = ((), (), s32[]{:S(2)}) async-start(), calls=%async_computation.17 | async-start | bytes 1622016
  2061.7 737.8 %reduce-scatter.15.cloned.1.call-start = ((), (), s32[]{:S(2)}) async-start(), calls=%async_computation.14 | async-start | bytes 1622016 | tf_op jit(solution)/shard_map/reduce_scatter | solution.py:362
  2066.8 325.8 %copy-start.140 = (u32[32]{0:T(128)S(1)}, u32[32]{0:T(128)}, u32[]{:S(2)}) copy-start(u32[32]{0:T(128)} %constant.925) | copy-start | bytes 388
  2066.8 327.1 %copy-start.124 = (f32[3072]{0:T(1024)S(1)}, f32[3072]{0:T(1024)}, u32[]{:S(2)}) copy-start(f32[3072]{0:T(1024)} %get-tuple-element.2862) | copy-start | bytes 36868
  2066.8 327.2 %copy-start.106 = (f32[3072]{0:T(1024)S(1)}, f32[3072]{0:T(1024)}, u32[]{:S(2)}) copy-start(f32[3072]{0:T(1024)} %get-tuple-element.2866) | copy-start | bytes 36868
  2066.8 327.2 %copy-start.107 = (f32[3072]{0:T(1024)S(1)}, f32[3072]{0:T(1024)}, u32[]{:S(2)}) copy-start(f32[3072]{0:T(1024)} %get-tuple-element.3384) | copy-start | bytes 36868
  2066.8 457.9 %copy-start.101 = (f32[3072]{0:T(1024)S(1)}, f32[3072]{0:T(1024)}, u32[]{:S(2)}) copy-start(f32[3072]{0:T(1024)} %get-tuple-element.2616) | copy-start | bytes 36868
  2066.9 520.1 %copy-start.8 = (bf16[1,256,1536]{2,1,0:T(8,128)(2,1)S(1)}, bf16[1,256,1536]{2,1,0:T(8,128)(2,1)}, u32[]{:S(2)}) copy-start(bf16[1,256,1536]{2,1,0:T(8,128)(2,1)} %param.59) | copy-start | bytes 2359300
  2066.9 520.1 %copy-start.42 = (bf16[1,256,3072]{2,1,0:T(8,128)(2,1)S(1)}, bf16[1,256,3072]{2,1,0:T(8,128)(2,1)}, u32[]{:S(2)}) copy-start(bf16[1,256,3072]{2,1,0:T(8,128)(2,1)} %get-tuple-element.3353) | copy-start | bytes 4718596
  2066.9 520.1 %copy-start.111 = (f32[1536]{0:T(1024)S(1)}, f32[1536]{0:T(1024)}, u32[]{:S(2)}) copy-start(f32[1536]{0:T(1024)} %copy-done.109) | copy-start | bytes 18436
  2066.9 786.4 %all-gather.13.cloned.1.call-start = ((), (), s32[]{:S(2)}) async-start(), calls=%async_computation.16 | async-start | bytes 2654208 | tf_op jit(solution)/shard_map/all_gather | solution.py:388
  2069.2 865.0 %all-gather.11.cloned.1.call-start = ((), (), s32[]{:S(2)}) async-start(), calls=%async_computation.13 | async-start | bytes 5308416 | tf_op jit(solution)/shard_map/all_gather | solution.py:385
  2594.4 10.0 copy-start.128
  2594.4 10.0 copy-start.117
  2594.4 10.6 copy-start.53
  (738 other events, 4952.3 us)
Sparse Core Ops, SparseCore 0:
  1522.2 206.9 reduce-scatter.16
  2040.2 350.1 reduce-scatter.12
  2396.5 96.1 reduce-scatter.20
  2498.7 96.1 reduce-scatter.22
  2600.8 96.0 reduce-scatter.18
  2703.4 96.0 reduce-scatter.14
  2801.9 51.3 all-gather.12
  2855.7 78.4 all-gather.10
where the time goes:
time: 2980 us; the launch traced here: 2950 us
  other arithmetic  893 us (30%)
  local copies, waits for them, and re-layouts  811 us (27%)
  waiting for transfers between devices  683 us (23%)
  matrix products  277 us (9%)
  blocking collectives  212 us (7%)
    reduce_scatter x1, waiting for transfers between devices, shards(): lax.psum_scatter(g_win, ('dp', 'seq'), scatter_dimension=0, tiled=True)  321 us
    reduce_sum x288, other arithmetic, step_block(): outputs.append(jnp.sum(carried * c_part[:, position, :, None], axis=1))  284 us
    squeeze x224, local copies, waits for them, and re-layouts, scan_local(): final, outputs = lax.scan(jax.checkpoint(step_block), start, pieces)  244 us
    unnamed x11, waiting for transfers between devices  171 us
    reduce_sum x128, other arithmetic, step_block(): decay = jnp.exp(d_part[:, position, None, :] * a_state)  123 us
    dot_general x32, matrix products, one_block(): jnp.einsum('ibne,ibe,ibn->ine', weight, g_part, c_part, precision=highest)  106 us
    another operation x64, local copies, waits for them, and re-layouts, step_block(): return (carried, jnp.stack(outputs, axis=1))  101 us
    mul x320, other arithmetic, step_block(): d_part[:, position] * v_part[:, position]  100 us
  transfers between devices with their start and end apart: 16, of which 8 were waited for; matrix products, arithmetic and copies ran while one was open for 31% of the time, Pallas kernels for 0%

commit v1 on v0

v1 whole, which is shorter than its diff:
```python
import jax
import jax.numpy as jnp
from jax import lax
from jax.experimental import pallas as pl
from jax.experimental.pallas import tpu as pltpu
from jax.sharding import PartitionSpec as P

epsilon = 1e-06
f32, bf16 = jnp.float32, jnp.bfloat16
LOG2E = 1.4426950408889634
CH = 16
N = 16
TB = 128

def dot(a, b): return lax.dot_general(a, b, (((1,), (0,)), ((), ())), preferred_element_type=f32)
def dot_t(a, b): return lax.dot_general(a, b, (((1,), (1,)), ((), ())), preferred_element_type=f32)

def scan_kernel(delta_ref, u_ref, bb_ref, cbd_ref, a2_ref, y_ref, s_ref, du_scr, st_scr):
    TB, C = delta_ref.shape
    L = C // 128
    i = pl.program_id(0)
    @pl.when(i == 0)
    def _():
        st_scr[...] = jnp.zeros_like(st_scr)
    du_scr[...] = delta_ref[...] * u_ref[...].astype(f32)
    s_ref[0, 0:N, :] = st_scr[...].astype(bf16)
    def chunk(k, st):
        base = pl.multiple_of(k * CH, CH)
        dref = delta_ref.at[pl.ds(base, CH), :]
        duref = du_scr.at[pl.ds(base, CH), :]
        bref = bb_ref.at[pl.ds(pl.multiple_of(base * N, CH * N), CH * N), :]
        sref = s_ref.at[0, pl.ds(pl.multiple_of(base * N + N, N), CH * N), :]
        st = list(st)
        for t in range(CH):
            b = bref[t * N:(t + 1) * N, :].astype(f32)
            for l in range(L):
                ls = slice(l * 128, (l + 1) * 128)
                d = jnp.broadcast_to(dref[t:t + 1, ls], (N, 128))
                w = jnp.broadcast_to(duref[t:t + 1, ls], (N, 128)) * b
                st[l] = jnp.exp2(d * a2_ref[:, ls]) * st[l] + w
                sref[t * N:(t + 1) * N, ls] = st[l].astype(bf16)
        y_ref[pl.ds(base, CH), :] = dot(cbd_ref[pl.ds(base, CH), :], sref[...])
        return tuple(st)
    st = tuple(st_scr[:, l * 128:(l + 1) * 128] for l in range(L))
    st = lax.fori_loop(0, TB // CH, chunk, st)
    for l in range(L):
        st_scr[:, l * 128:(l + 1) * 128] = st[l]

def scan_forward(delta, u, bb, cbd, a2):
    T, C = delta.shape
    nb = T // TB
    return pl.pallas_call(
        scan_kernel, grid=(nb,),
        in_specs=[pl.BlockSpec((TB, C), lambda i: (i, 0)), pl.BlockSpec((TB, C), lambda i: (i, 0)),
                  pl.BlockSpec((TB * N, 128), lambda i: (i, 0)), pl.BlockSpec((TB, CH * N), lambda i: (i, 0)),
                  pl.BlockSpec((N, C), lambda i: (0, 0))],
        out_specs=[pl.BlockSpec((TB, C), lambda i: (i, 0)), pl.BlockSpec((1, (TB + 1) * N, C), lambda i: (i, 0, 0))],
        out_shape=[jax.ShapeDtypeStruct((T, C), f32), jax.ShapeDtypeStruct((nb, (TB + 1) * N, C), bf16)],
        scratch_shapes=[pltpu.VMEM((TB, C), f32), pltpu.VMEM((N, C), f32)],
        compiler_params=pltpu.CompilerParams(vmem_limit_bytes=48 << 20),
        name="scan_out",
    )(delta, u, bb, cbd, a2)

def adjoint_kernel(delta_ref, u_ref, g_ref, cb_ref, bbd_ref, a2_ref, a_ref, sum_ref, s_ref,
               dd_ref, du_ref, db_ref, dc_ref, da_ref, dux, lam, ra, rd, dl_scr):
    TB, C = delta_ref.shape
    L = C // 128
    i = pl.program_id(0)
    @pl.when(i == 0)
    def _():
        dl_scr[...] = jnp.zeros_like(dl_scr)
        da_ref[...] = jnp.zeros_like(da_ref)
    dux[...] = (delta_ref[...] * u_ref[...].astype(f32)).astype(bf16)
    pick = (lax.broadcasted_iota(jnp.int32, (CH, CH * N), 1) // N == lax.broadcasted_iota(jnp.int32, (CH, CH * N), 0))
    def chunk(kk, dl):
        k = TB // CH - 1 - kk
        base = pl.multiple_of(k * CH, CH)
        rows = pl.ds(base, CH)
        dref = delta_ref.at[rows, :]
        gref = g_ref.at[rows, :]
        cref = cb_ref.at[pl.ds(pl.multiple_of(base * N, CH * N), CH * N), :]
        pref = s_ref.at[0, pl.ds(pl.multiple_of(base * N, N), CH * N), :]
        sref = s_ref.at[0, pl.ds(pl.multiple_of(base * N + N, N), CH * N), :]
        dl = list(dl)
        for t in reversed(range(CH)):
            rs = slice(t * N, (t + 1) * N)
            c = cref[rs, :].astype(f32)
            for l in range(L):
                ls = slice(l * 128, (l + 1) * 128)
                d = jnp.broadcast_to(dref[t:t + 1, ls], (N, 128))
                g = jnp.broadcast_to(gref[t:t + 1, ls], (N, 128)).astype(f32)
                lm = dl[l] + g * c
                dl[l] = jnp.exp2(d * a2_ref[:, ls]) * lm
                lam[rs, ls] = lm.astype(bf16)
                r = dl[l].astype(bf16) * pref[rs, ls]
                ra[rs, ls] = r * a_ref[:, ls]
                rd[rs, ls] = r * d.astype(bf16)
        ddu = dot(bbd_ref[rows, :], lam[...])
        dda = dot(sum_ref[0:CH, :], ra[...])
        da_ref[...] += dot(sum_ref[CH:2 * CH, :], rd[...])
        dbm = dot_t(dux[rows, :], lam[...])
        dcm = dot_t(gref[...].astype(bf16), sref[...])
        db_ref[k] = jnp.sum(jnp.where(pick, dbm, 0.0), axis=0, keepdims=True)
        dc_ref[k] = jnp.sum(jnp.where(pick, dcm, 0.0), axis=0, keepdims=True)
        dd_ref[rows, :] = dda + u_ref[rows, :].astype(f32) * ddu
        du_ref[rows, :] = (dref[...] * ddu).astype(du_ref.dtype)
        return tuple(dl)
    dl = tuple(dl_scr[:, l * 128:(l + 1) * 128] for l in range(L))
    dl = lax.fori_loop(0, TB // CH, chunk, dl)
    for l in range(L):
        dl_scr[:, l * 128:(l + 1) * 128] = dl[l]

def scan_adjoint(delta, u, g, cb, bbd, a2, a16, S, du_dtype=f32):
    T, C = delta.shape
    nb = T // TB
    q = jnp.arange(CH * N)
    sums = jnp.concatenate([(q[None, :] // N == jnp.arange(CH)[:, None]), (q[None, :] % N == jnp.arange(N)[:, None])]).astype(bf16)
    rev = lambda i: (nb - 1 - i, 0)
    rev3 = lambda i: (nb - 1 - i, 0, 0)
    zero = lambda i: (0, 0)
    return pl.pallas_call(
        adjoint_kernel, grid=(nb,),
        in_specs=[pl.BlockSpec((TB, C), rev), pl.BlockSpec((TB, C), rev), pl.BlockSpec((TB, C), rev),
                  pl.BlockSpec((TB * N, 128), rev), pl.BlockSpec((TB, CH * N), rev),
                  pl.BlockSpec((N, C), zero), pl.BlockSpec((N, C), zero), pl.BlockSpec((2 * CH, CH * N), zero),
                  pl.BlockSpec((1, (TB + 1) * N, C), rev3)],
        out_specs=[pl.BlockSpec((TB, C), rev), pl.BlockSpec((TB, C), rev),
                   pl.BlockSpec((TB // CH, 1, CH * N), rev3), pl.BlockSpec((TB // CH, 1, CH * N), rev3),
                   pl.BlockSpec((N, C), zero)],
        out_shape=[jax.ShapeDtypeStruct((T, C), f32), jax.ShapeDtypeStruct((T, C), du_dtype),
                   jax.ShapeDtypeStruct((T // CH, 1, CH * N), f32), jax.ShapeDtypeStruct((T // CH, 1, CH * N), f32),
                   jax.ShapeDtypeStruct((N, C), f32)],
        scratch_shapes=[pltpu.VMEM((TB, C), bf16), pltpu.VMEM((CH * N, C), bf16), pltpu.VMEM((CH * N, C), bf16),
                        pltpu.VMEM((CH * N, C), bf16), pltpu.VMEM((N, C), f32)],
        compiler_params=pltpu.CompilerParams(vmem_limit_bytes=48 << 20),
        name="scan_back",
    )(delta, u, g, cb, bbd, a2, a16, sums, S)

def blockdiag(m):
    T = m.shape[0]
    tl = jnp.tile(m, (1, CH))
    keep = (jnp.arange(CH * N)[None, :] // N) == (jnp.arange(T)[:, None] % CH)
    return jnp.where(keep, tl, 0).astype(bf16)
def lanes(m):
    T = m.shape[0]
    return jnp.broadcast_to(m.reshape(T * N, 1), (T * N, 128)).astype(bf16)


def silu_slope(value):
    sigmoid = jax.nn.sigmoid(value)
    return sigmoid * (1.0 + value * (1.0 - sigmoid))


def normalize(rows_in, shift, scale):
    mean = jnp.mean(rows_in, axis=-1, keepdims=True)
    centered = rows_in - mean
    variance = jnp.mean(centered * centered, axis=-1, keepdims=True)
    return centered * lax.rsqrt(variance + epsilon) * (1.0 + scale) + shift


def partner(block, axis, bit):
    return lax.ppermute(block, axis, [(i, i ^ bit) for i in range(lax.axis_size(axis))])


def bits_down(axis):
    bit = lax.axis_size(axis) // 2
    while bit:
        yield bit
        bit //= 2


def bits_up(axis):
    return reversed(list(bits_down(axis)))


def gather_rows(block, axis, bits):
    index = lax.axis_index(axis)
    size = lax.axis_size(axis)
    held = block[(None,) * len(bits)]
    places = [b.bit_length() - 1 for b in bits]
    for bit, place in zip(bits, places):
        other = partner(held, axis, bit)
        dim = len(bits) - 1 - place
        upper = (index & bit) != 0
        held = jnp.concatenate([jnp.where(upper, other, held), jnp.where(upper, held, other)], axis=dim)
    return held.reshape((size,) + block.shape)


def scatter_sum(blocks, axis, bits):
    index = lax.axis_index(axis)
    count = len(bits)
    held = blocks.reshape((2,) * count + blocks.shape[1:])
    for bit in bits:
        dim = count - 1 - (bit.bit_length() - 1)
        mine = (index & bit) // bit
        keep = lax.dynamic_index_in_dim(held, mine, dim, keepdims=True)
        send = lax.dynamic_index_in_dim(held, 1 - mine, dim, keepdims=True).astype(bf16)
        held = keep.astype(f32) + partner(send, axis, bit).astype(f32)
    return held.reshape(blocks.shape[1:])


def sum_seq(value):
    index = lax.axis_index("seq")
    rows = value.shape[0] // 2
    halves = value.reshape((2, rows) + value.shape[1:])
    mine = index & 1
    held = lax.dynamic_index_in_dim(halves, mine, 0, keepdims=False) + partner(
        lax.dynamic_index_in_dim(halves, 1 - mine, 0, keepdims=False), "seq", 1
    )
    bit = 2
    while bit < lax.axis_size("seq"):
        held = held + partner(held, "seq", bit)
        bit *= 2
    other = partner(held, "seq", 1)
    upper = mine != 0
    return jnp.concatenate([jnp.where(upper, other, held), jnp.where(upper, held, other)], axis=0)


def across_seq(blocks):
    return lax.all_to_all(blocks, "seq", split_axis=0, concat_axis=0, tiled=True)


def contract_rows(left, right):
    return lax.dot_general(left, right, (((0,), (0,)), ((), ())), preferred_element_type=f32)


def diagonal_rows(value):
    return value.reshape(-1, N)


def shards(
    tokens,
    modulation,
    heights,
    w_in,
    w_x,
    w_dt,
    b_dt,
    a_log,
    d_skip,
    conv_w,
    conv_b,
    w_out,
    cotangent,
):
    _, seq_len, width = tokens.shape
    parts = lax.axis_size("seq")
    data_parts = lax.axis_size("dp")
    inner = w_out.shape[0]
    chans = inner // parts
    rank = w_dt.shape[1]
    taps = conv_w.shape[1]
    total = seq_len * parts
    part = lax.axis_index("seq")
    seq_down, seq_up = list(bits_down("seq")), list(bits_up("seq"))
    dp_down, dp_up = list(bits_down("dp")), list(bits_up("dp"))

    def own(array, axis=0, offset=0):
        return lax.dynamic_slice_in_dim(array, offset + part * chans, chans, axis)

    w_conv_in, w_gate_in = own(w_in, 1), own(w_in, 1, inner)
    wx, wdt, bdt, wout = own(w_x), own(w_dt), own(b_dt), own(w_out)
    dsk, cw, cb = own(d_skip), own(conv_w), own(conv_b)
    a_state = -jnp.exp(own(a_log).T)
    a_two = a_state * LOG2E
    a_low = a_state.astype(bf16)
    shift, scale, gate = modulation[0, 0:1], modulation[0, 1:2], modulation[0, 2:3]

    x_own = tokens[0].astype(f32)
    normed, norm_back = jax.vjp(lambda rows_in: normalize(rows_in, shift, scale), x_own)
    hmod = gather_rows(normed.astype(bf16), "seq", seq_down).reshape(total, width)
    d_res = cotangent[0].astype(f32)
    d_branch = gather_rows((gate * d_res).astype(bf16), "seq", seq_down).reshape(total, width)

    x_conv = dot(hmod, w_conv_in).astype(bf16)
    z_gate = dot(hmod, w_gate_in)
    padded = jnp.concatenate([jnp.zeros((taps - 1, chans), bf16), x_conv], axis=0).astype(f32)
    pre_conv = cb + sum(padded[k : k + total] * cw[:, k] for k in range(taps))
    u_low = jax.nn.silu(pre_conv).astype(bf16)
    proj = sum_seq(dot(u_low, wx)).astype(bf16)

    height = heights[0]
    wide = total // height
    column = total - 1 - jnp.arange(total, dtype=jnp.int32)
    order = column % height * wide + column // height
    to_columns = (order[:, None] == jnp.arange(total, dtype=jnp.int32)[None, :]).astype(bf16)

    def columns_of(value):
        return dot(to_columns, value).astype(bf16)

    def rows_of(value):
        return contract_rows(to_columns, value)

    u_col = columns_of(u_low)
    proj_col = columns_of(proj)

    def terms(p):
        pre = dot_t(p[:, :rank], wdt) + bdt
        b_mat, c_mat = p[:, rank : rank + N], p[:, rank + N :]
        return (jax.nn.softplus(pre), lanes(b_mat), lanes(c_mat), blockdiag(b_mat), blockdiag(c_mat))

    delta_row, bl_row, cl_row, bd_row, cd_row = terms(proj)
    delta_col, bl_col, cl_col, bd_col, cd_col = terms(proj_col)
    y_fwd, s_row = scan_forward(delta_row, u_low, bl_row, cd_row, a_two)
    y_col, s_col = scan_forward(delta_col, u_col, bl_col, cd_col, a_two)
    u_full = u_low.astype(f32)
    y_all = y_fwd + rows_of(y_col.astype(bf16)) + dsk * u_full
    silu_z = jax.nn.silu(z_gate)
    gated = (y_all * silu_z).astype(bf16)
    branch = scatter_sum(dot(gated, wout).astype(bf16).reshape(parts, seq_len, width), "seq", seq_up)
    result = (x_own + gate * branch).astype(bf16)

    d_gated = dot_t(d_branch, wout)
    d_y = d_gated * silu_z
    d_z = (d_gated * y_all * silu_slope(z_gate)).astype(bf16)
    g_dskip = jnp.sum(d_y * u_full, axis=0)
    g_out = contract_rows(gated, d_branch).astype(bf16)
    g_gate = contract_rows(hmod, d_z).astype(bf16)

    def by_owner(grad):
        shaped = grad.reshape(parts, data_parts, width // (parts * data_parts), chans)
        return shaped.swapaxes(0, 1)

    out_sum = lax.psum_scatter(g_out, "dp", scatter_dimension=0, tiled=True)
    g_out = lax.all_gather(out_sum.astype(bf16), "dp", axis=0, tiled=True).astype(f32)
    gate_sum = lax.psum_scatter(by_owner(g_gate), "dp", scatter_dimension=0, tiled=True)[0]
    gate_sum = across_seq(gate_sum.astype(bf16)).swapaxes(0, 1)
    g_gate = lax.all_gather(gate_sum, "dp", axis=0, tiled=True).reshape(width // parts, inner).astype(f32)

    dy_col = columns_of(d_y.astype(bf16))
    dd_col, du_col, db_col, dc_col, da_col = scan_adjoint(
        delta_col, u_col, dy_col, cl_col, bd_col, a_two, a_low, s_col, bf16
    )
    dd_row, du_row, db_row, dc_row, da_row = scan_adjoint(
        delta_row, u_low, d_y, cl_row, bd_row, a_two, a_low, s_row, f32
    )

    def low_grads(dd, delta, p, db, dc):
        d_pre = dd * -jnp.expm1(-delta)
        low_pre = d_pre.astype(bf16)
        grad = jnp.concatenate([dot(low_pre, wdt), diagonal_rows(db), diagonal_rows(dc)], axis=1)
        return grad, contract_rows(low_pre, p[:, :rank]), jnp.sum(d_pre, axis=0)

    p_col, gw_col, gb_col = low_grads(dd_col, delta_col, proj_col, db_col, dc_col)
    p_row, gw_row, gb_row = low_grads(dd_row, delta_row, proj, db_row, dc_row)
    d_projs = sum_seq(jnp.concatenate([p_row, p_col], axis=1))
    d_proj = (d_projs[:, : p_row.shape[1]] + rows_of(d_projs[:, p_row.shape[1] :].astype(bf16))).astype(bf16)
    g_wx = contract_rows(u_low, d_proj)
    d_u = du_row + rows_of(du_col) + d_y * dsk + dot_t(d_proj, wx)
    d_pre_conv = d_u * silu_slope(pre_conv)
    g_convb = jnp.sum(d_pre_conv, axis=0)
    g_convw = jnp.stack(
        [jnp.sum(padded[k : k + total] * d_pre_conv, axis=0) for k in range(taps)], axis=1
    )
    later = jnp.concatenate([d_pre_conv, jnp.zeros((taps - 1, chans), f32)], axis=0)
    d_xconv = sum(cw[:, k] * later[taps - 1 - k : taps - 1 - k + total] for k in range(taps)).astype(bf16)

    g_conv_in = by_owner(contract_rows(hmod, d_xconv).astype(bf16))
    rows_each = parts * g_conv_in.shape[2]
    small = jnp.concatenate(
        [
            g_wx,
            gw_row + gw_col,
            ((da_row + da_col) * a_state).T,
            (gb_row + gb_col)[:, None],
            g_dskip[:, None],
            g_convb[:, None],
            g_convw,
        ],
        axis=1,
    )
    columns = small.shape[1]
    small = jnp.pad(small, ((0, 0), (0, -columns % 128))).astype(bf16)
    small = small.reshape(data_parts, -1, chans)
    payload = jnp.concatenate([g_conv_in.reshape(data_parts, rows_each, chans), small], axis=1)
    held = scatter_sum(payload, "dp", dp_up).astype(bf16)
    mine = across_seq(held[:rows_each].reshape(parts, -1, chans)).swapaxes(0, 1)
    held = jnp.concatenate([mine.reshape(rows_each, chans), held[rows_each:]], axis=0)
    held = gather_rows(held, "dp", dp_down)
    g_conv_in = held[:, :rows_each].reshape(width // parts, inner).astype(f32)
    small = held[:, rows_each:].reshape(chans, -1).astype(f32)

    d_h = dot_t(d_xconv, w_conv_in) + dot_t(d_z, w_gate_in)
    d_h = scatter_sum(d_h.astype(bf16).reshape(parts, seq_len, width), "seq", seq_up)
    d_x = d_res + norm_back(d_h)[0]

    edges = [0]
    for size in (w_x.shape[1], rank, N, 1, 1, 1, taps):
        edges.append(edges[-1] + size)
    pieces = [small[:, lo:hi] for lo, hi in zip(edges, edges[1:])]
    return (
        result[None],
        d_x[None],
        jnp.concatenate([g_conv_in, g_gate], axis=1),
        pieces[0],
        pieces[1],
        pieces[3][:, 0],
        pieces[2],
        pieces[4][:, 0],
        pieces[6],
        pieces[5][:, 0],
        g_out,
    )


def solution(mesh):
    placed = (
        P("dp", "seq", None),
        P("dp", None, None),
        P("dp"),
        P(),
        P(),
        P(),
        P(),
        P(),
        P(),
        P(),
        P(),
        P(),
        P("dp", "seq", None),
    )
    return jax.shard_map(
        shards,
        mesh=mesh,
        in_specs=placed,
        out_specs=(
            P("dp", "seq", None),
            P("dp", "seq", None),
            P("seq", None),
            P("seq", None),
            P("seq", None),
            P("seq"),
            P("seq", None),
            P("seq"),
            P("seq", None),
            P("seq"),
            P("seq", None),
        ),
        check_vma=False,
    )
```

time: 2980 us -> 674 us (0.23)
  other arithmetic: 893 us -> 57.7 us
  local copies, waits for them, and re-layouts: 811 us -> 80.9 us
  waiting for transfers between devices: 683 us -> 234 us
  blocking collectives: 212 us -> 0 us
  matrix products: 277 us -> 98.9 us
  Pallas kernels: 0 us -> 154 us
    reduce_sum x418 -> x4, other arithmetic: 423 us -> 10.5 us  [the longest x2 6.19 us: low_grads(): return (grad, contract_rows(low_pre, p[:, :rank]), jnp.sum(d_pre, axis=0))]
    reduce_scatter x3 -> x1, waiting for transfers between devices: 391 us -> 0.01 us  [shards(): out_sum = lax.psum_scatter(g_out, 'dp', scatter_dimension=0, tiled=True)]
    squeeze x224 -> x2, local copies, waits for them, and re-layouts: 244 us -> 2.37 us  [the longest x1 2.34 us: shards(): lax.psum_scatter(by_owner(g_gate), 'dp', scatter_dimension=0, tiled=True)[0]]
    another operation x183 -> x12, local copies, waits for them, and re-layouts: 192 us -> 4.27 us  [the longest x8 4.25 us: blockdiag(): tl = jnp.tile(m, (1, CH))]
    dot_general x76 -> x15, matrix products: 252 us -> 65 us  [the longest x6 35 us: dot_t(): lax.dot_general(a, b, (((1,), (1,)), ((), ())), preferred_element_type=f32)]
    pallas_call x0 -> x4, Pallas kernels: none -> 154 us  [the longest x2 103 us: scan_adjoint(): pl.pallas_call(adjoint_kernel, grid=(nb,), in_specs=[pl.BlockSpec((TB, C)...]
    all_gather x10 -> x0, blocking collectives: 153 us -> none  [the longest x6 44.3 us: carried_in(): lax.all_gather(part.astype(kind), axis)]
    ppermute x2 -> x20, waiting for transfers between devices: 0.01 us -> 151 us  [partner(): lax.ppermute(block, axis, [(i, i ^ bit) for i in range(lax.axis_size(axis...]
  transfers between devices with their start and end apart: 16 -> 26, of which waited for: 8 -> 13; matrix products, arithmetic and copies ran while one was open for 31% -> 21% of each run, Pallas kernels for 0% -> 0%
where the time goes in v1:
time: 674 us; the launch traced here: 665 us
  waiting for transfers between devices  234 us (35%)
  Pallas kernels  154 us (23%)
  matrix products  98.9 us (15%)
  local copies, waits for them, and re-layouts  80.9 us (12%)
  other arithmetic  57.7 us (9%)
  starting transfers between devices  23.7 us (4%)
  between operations  16.2 us (2%)
    ppermute x20, waiting for transfers between devices, partner(): lax.ppermute(block, axis, [(i, i ^ bit) for i in range(lax.axis_size(axis...  151 us
    pallas_call x2, Pallas kernels, scan_adjoint(): pl.pallas_call(adjoint_kernel, grid=(nb,), in_specs=[pl.BlockSpec((TB, C)...  103 us
    unnamed x5, waiting for transfers between devices  58.4 us
    pallas_call x2, Pallas kernels, scan_forward(): pl.pallas_call(scan_kernel, grid=(nb,), in_specs=[pl.BlockSpec((TB, C), l...  50.4 us
    dot_general x6, matrix products, dot_t(): lax.dot_general(a, b, (((1,), (1,)), ((), ())), preferred_element_type=f32)  35 us
    dot_general x9, matrix products, contract_rows(): lax.dot_general(left, right, (((0,), (0,)), ((), ())), preferred_element_...  33.9 us
    dot_general x9, matrix products, dot(): lax.dot_general(a, b, (((1,), (0,)), ((), ())), preferred_element_type=f32)  30 us
    all_gather x1, waiting for transfers between devices, shards(): lax.all_gather(out_sum.astype(bf16), 'dp', axis=0, tiled=True).astype(f32)  18.8 us
  transfers between devices with their start and end apart: 26, of which 13 were waited for; matrix products, arithmetic and copies ran while one was open for 21% of the time, Pallas kernels for 0%

profile of v1, /device:TPU:0, one launch (start us, length us, event | category | flops | bytes accessed | tf_op | source)
XLA Modules:
  0.0 665.3 jit_solution(13854964283083452391)
XLA Ops:
  11.1 2.4 fusion.47
  13.4 3.0 collective-permute-start
  17.4 17.6 %collective-permute-done = bf16[1,1,256,1536]{3,2,1,0:T(8,128)(2,1)S(1)} collective-permute-done((bf16[1,1,256,1536]{3,2,1,0:T(8,128)(2,1)}, bf16[1,1,256,1536]{3,2,1,0:T(8,128)(2,1)S(1)}, u32[]{:S(2)}, u32[]{:S(2)}) %collective-permute-start) | collective-permute-done | bytes 786464 | tf_op jit(solution)/shard_map/ppermute | solution.py:162
  35.9 15.2 %collective-permute-done.7 = bf16[1,1,256,1536]{3,2,1,0:T(8,128)(2,1)} collective-permute-done((bf16[1,1,256,1536]{3,2,1,0:T(8,128)(2,1)}, bf16[1,1,256,1536]{3,2,1,0:T(8,128)(2,1)}, u32[]{:S(2)}, u32[]{:S(2)}) %collective-permute-start.7) | collective-permute-done | bytes 786464 | tf_op jit(solution)/shard_map/ppermute | solution.py:162
  51.1 2.5 broadcast_select_fusion.7
  61.6 5.4 fusion.26
  67.3 5.4 fusion.20
  74.4 9.3 %fusion.7 = (bf16[768]{0:T(1024)(128)(2,1)S(1)}, f32[1024,768]{1,0:T(8,128)}, bf16[1024,768]{1,0:T(8,128)(2,1)S(1)}, f32[1024,768]{1,0:T(8,128)}, f32[1024,768]{1,0:T(8,128)}) fusion(f32[1024,768]{1,0:T(8,128)S(1)} %fusion.20, f32[768]{0:T(1024)S(1)} %get-tuple-element.127, f32[1027,768]{1,0:T(8,128)S(1)} %pad_convert_fusion, ...), kind=kOutput, calls=%fused_computation.20 | convolution fusion | flops 2432433408 | bytes 32260612 | tf_op jit(solution)/shard_map/dot_general | solution.py:16
  88.5 1.8 collective-permute-start.3
  90.3 5.0 fusion.30.g_ref
  95.3 1.8 collective-permute-done.3
  97.3 3.1 fusion.29.u_ref
  100.5 1.7 fusion.55
  103.5 4.5 compare_select_fusion.delta_ref
  108.0 4.5 compare_select_fusion.1.delta_ref
  119.9 1.8 compare_select_fusion.2
  121.7 3.8 broadcast_in_dim.41.bb_ref
  125.5 25.2 %scan_out.3 = (f32[1024,768]{1,0:T(8,128)S(1)}, bf16[8,2064,768]{2,1,0:T(8,128)(2,1)}) custom-call(f32[1024,768]{1,0:T(8,128)} %compare_select_fusion.delta_ref, bf16[1024,768]{1,0:T(8,128)(2,1)S(1)} %copy-done.1, bf16[16384,128]{1,0:T(8,128)(2,1)} %broadcast_in_dim.41.bb_ref, bf16[1024,256]{1,0:T(8,128)(2,1)S(1)} %get-tuple-element.170.cbd_ref, ...), custom_call_target="tpu_custom_call" | custom-call | tf_op jit(solution)/shard_map/scan_out/pallas_call | solution.py:52
  152.4 3.8 broadcast_in_dim.45.cb_ref
  156.2 52.6 %scan_back.3 = (f32[1024,768]{1,0:T(8,128)}, bf16[1024,768]{1,0:T(8,128)(2,1)S(1)}, f32[64,1,256]{2,1,0:T(1,128)S(1)}, f32[64,1,256]{2,1,0:T(1,128)S(1)}, f32[16,768]{1,0:T(8,128)S(1)}) custom-call(f32[1024,768]{1,0:T(8,128)} %compare_select_fusion.delta_ref, bf16[1024,768]{1,0:T(8,128)(2,1)S(1)} %copy-done.1, bf16[1024,768]{1,0:T(8,128)(2,1)S(1)} %copy-done.2, ...), custom_call_target="tpu_custom_call" | custom-call | tf_op jit(solution)/shard_map/scan_back/pallas_call | solution.py:121
  208.8 3.8 fusion.59
  212.5 3.8 broadcast_in_dim.38.bb_ref
  216.3 25.2 %scan_out.2 = (f32[1024,768]{1,0:T(8,128)S(1)}, bf16[8,2064,768]{2,1,0:T(8,128)(2,1)}) custom-call(f32[1024,768]{1,0:T(8,128)} %compare_select_fusion.1.delta_ref, bf16[1024,768]{1,0:T(8,128)(2,1)S(1)} %get-tuple-element.133.u_ref, bf16[16384,128]{1,0:T(8,128)(2,1)} %broadcast_in_dim.38.bb_ref, bf16[1024,256]{1,0:T(8,128)(2,1)S(1)} %get-tuple-element.171.cbd_ref, ...), custom_call_target="tpu_custom_call" | custom-call | tf_op jit(solution)/shard_map/scan_out/pallas_call | solution.py:52
  243.2 3.8 broadcast_in_dim.43.cb_ref
  246.9 50.5 %scan_back.2 = (f32[1024,768]{1,0:T(8,128)S(1)}, f32[1024,768]{1,0:T(8,128)}, f32[64,1,256]{2,1,0:T(1,128)S(1)}, f32[64,1,256]{2,1,0:T(1,128)S(1)}, f32[16,768]{1,0:T(8,128)S(1)}) custom-call(f32[1024,768]{1,0:T(8,128)} %compare_select_fusion.1.delta_ref, bf16[1024,768]{1,0:T(8,128)(2,1)S(1)} %get-tuple-element.133.u_ref, ...), custom_call_target="tpu_custom_call" | custom-call | tf_op jit(solution)/shard_map/scan_back/pallas_call | solution.py:121
  297.5 2.4 fusion.57
  302.5 2.8 fusion.79
  309.6 9.1 %multiply_convert_fusion = (bf16[1024,768]{1,0:T(8,128)(2,1)S(1)}, bf16[1024,768]{1,0:T(8,128)(2,1)}) fusion(f32[1024,768]{1,0:T(8,128)} %copy-done.54, f32[1024,768]{1,0:T(8,128)} %get-tuple-element.172, bf16[1024,768]{1,0:T(8,128)(2,1)S(1)} %get-tuple-element.133.u_ref, f32[768]{0:T(1024)S(1)} %copy-done.45, f32[1024,768]{1,0:T(8,128)} %copy-done.4, ...), kind=kOutput, calls=%fused_computation.28 | convolution fusion | flops 1625817088 | bytes 17308672 | tf_op jit(solution)/shard_map/dot_general | solution.py:224
  318.7 4.2 convolution_convert_fusion.2
  326.2 2.7 constant_dynamic-slice_fusion.3
  330.6 2.6 fusion.114
  333.7 5.6 fusion.1
  340.3 1.8 collective-permute-start.10
  342.1 4.0 convolution_convert_fusion.1
  346.1 8.2 %collective-permute-done.10 = f32[512,256]{1,0:T(8,128)} collective-permute-done((f32[512,256]{1,0:T(8,128)S(1)}, f32[512,256]{1,0:T(8,128)}, u32[]{:S(2)}, u32[]{:S(2)}) %collective-permute-start.10) | collective-permute-done | bytes 524320 | tf_op jit(solution)/shard_map/ppermute | solution.py:162
  356.4 2.1 fusion.56
  361.3 4.6 multiply_multiply_fusion
  365.9 3.9 multiply_reduce_fusion
  371.7 4.6 convolution_convert_fusion.3
  377.6 1.7 collective-permute-start.14
  379.9 58.4 %all-reduce.6.cloned.1.call-done = bf16[8,4,48,768]{3,2,0,1:T(8,128)(2,1)} async-done(((bf16[8,4,48,768]{3,2,0,1:T(8,128)(2,1)}), bf16[8,4,48,768]{3,2,0,1:T(8,128)(2,1)}) %all-reduce.6.cloned.1.call-update) | async-done | bytes 2359312
  438.3 2.3 dynamic-slice_bitcast_fusion
  440.7 4.1 all-to-all-start.1
  444.8 7.5 %fusion.22 = f32[1024,1536]{1,0:T(8,128)} fusion(bf16[1024,768]{1,0:T(8,128)(2,1)} %get-tuple-element.141, bf16[1536,6144]{1,0:T(8,128)(2,1)} %param.16, s32[]{:T(128)S(6)} %select_n.288), kind=kOutput, calls=%fused_computation.65 | convolution fusion | flops 2415919104 | bytes 10223620 | tf_op jit(solution)/shard_map/dot_general | solution.py:16
  452.3 1.8 copy.157
  454.2 1.8 convert_add_fusion.3
  457.8 4.6 add_convert_fusion
  464.2 21.6 %collective-permute-done.15 = bf16[2,1,1,224,768]{4,3,2,1,0:T(8,128)(2,1)S(1)} collective-permute-done((bf16[2,1,1,224,768]{4,3,2,1,0:T(8,128)(2,1)S(1)}, bf16[2,1,1,224,768]{4,3,2,1,0:T(8,128)(2,1)S(1)}, u32[]{:S(2)}, u32[]{:S(2)}) %collective-permute-start.15) | collective-permute-done | bytes 688160 | tf_op jit(solution)/shard_map/ppermute | solution.py:162
  487.6 4.5 convolution_convert_fusion
  493.5 10.9 %collective-permute-done.16 = bf16[1,1,1,224,768]{4,3,2,1,0:T(8,128)(2,1)S(1)} collective-permute-done((bf16[1,1,1,224,768]{4,3,2,1,0:T(8,128)(2,1)S(1)}, bf16[1,1,1,224,768]{4,3,2,1,0:T(8,128)(2,1)S(1)}, u32[]{:S(2)}, u32[]{:S(2)}) %collective-permute-start.16) | collective-permute-done | bytes 344096 | tf_op jit(solution)/shard_map/ppermute | solution.py:162
  505.2 3.5 all-to-all-start
  509.0 6.0 all-to-all-done
  515.4 2.4 convert_add_fusion
  520.0 13.1 %collective-permute-done.17 = bf16[1,1,1,224,768]{4,3,2,1,0:T(8,128)(2,1)S(1)} collective-permute-done((bf16[1,1,1,224,768]{4,3,2,1,0:T(8,128)(2,1)S(1)}, bf16[1,1,1,224,768]{4,3,2,1,0:T(8,128)(2,1)S(1)}, u32[]{:S(2)}, u32[]{:S(2)}) %collective-permute-start.17) | collective-permute-done | bytes 344096 | tf_op jit(solution)/shard_map/ppermute | solution.py:162
  534.2 2.5 convert_add_fusion.1
  538.0 23.2 %collective-permute-done.18 = bf16[2,1,1,224,768]{4,3,2,1,0:T(8,128)(2,1)} collective-permute-done((bf16[2,1,1,224,768]{4,3,2,1,0:T(8,128)(2,1)}, bf16[2,1,1,224,768]{4,3,2,1,0:T(8,128)(2,1)}, u32[]{:S(2)}, u32[]{:S(2)}) %collective-permute-start.18) | collective-permute-done | bytes 688160 | tf_op jit(solution)/shard_map/ppermute | solution.py:162
  565.2 2.3 convert_add_fusion.4
  567.6 38.8 %collective-permute-done.19 = bf16[2,2,1,224,768]{4,3,2,1,0:T(8,128)(2,1)S(1)} collective-permute-done((bf16[2,2,1,224,768]{4,3,2,1,0:T(8,128)(2,1)S(1)}, bf16[2,2,1,224,768]{4,3,2,1,0:T(8,128)(2,1)S(1)}, u32[]{:S(2)}, u32[]{:S(2)}) %collective-permute-start.19) | collective-permute-done | bytes 1376288 | tf_op jit(solution)/shard_map/ppermute | solution.py:162
  609.8 4.9 convert_element_type.246
  618.4 5.3 copy.158
  623.7 4.4 copy.159
  628.2 6.9 %maximum_convert_fusion = f32[384,6144]{1,0:T(8,128)} fusion(bf16[384,3072]{1,0:T(8,128)(2,1)} %copy.159, bf16[384,3072]{1,0:T(8,128)(2,1)S(1)} %copy-done.15), kind=kLoop, calls=%fused_computation.3 | loop fusion | flops 9437184 | bytes 14155776 | tf_op jit(solution)/shard_map/concatenate | solution.py:394
  635.0 18.8 %all-gather.5.cloned.1.call-done = bf16[768,1536]{1,0:T(8,128)(2,1)} async-done(((bf16[96,1536]{1,0:T(8,128)(2,1)}), bf16[768,1536]{1,0:T(8,128)(2,1)}) %all-gather.5.cloned.1.call-update) | async-done | bytes 2359312 | tf_op jit(solution)/shard_map/all_gather | solution.py:325
  653.8 4.5 convert_element_type.252
  (278 shorter events, 77.3 us)
Async XLA Ops:
  7.2 76.6 %copy-start = (bf16[3072,128]{1,0:T(8,128)(2,1)S(1)}, bf16[3072,128]{1,0:T(8,128)(2,1)}, u32[]{:S(2)}) copy-start(bf16[3072,128]{1,0:T(8,128)(2,1)} %param.17) | copy-start | bytes 2359300
  7.2 43.9 %copy-start.8 = (bf16[1,256,1536]{2,1,0:T(8,128)(2,1)S(1)}, bf16[1,256,1536]{2,1,0:T(8,128)(2,1)}, u32[]{:S(2)}) copy-start(bf16[1,256,1536]{2,1,0:T(8,128)(2,1)} %param.13) | copy-start | bytes 2359300
  7.2 9.2 %copy-start.20 = (bf16[1,256,1536]{2,1,0:T(8,128)(2,1)S(1)}, bf16[1,256,1536]{2,1,0:T(8,128)(2,1)}, u32[]{:S(2)}) copy-start(bf16[1,256,1536]{2,1,0:T(8,128)(2,1)} %param.25) | copy-start | bytes 2359300
  7.2 431.1 %all-reduce.6.cloned.1.call-start = ((), (), s32[]{:S(2)}) async-start(), calls=%async_computation.6 | async-start | bytes 4718592
  8.7 44.9 %copy-start.39 = (f32[256]{0:T(256)}, f32[256]{0:T(256)S(1)}, u32[]{:S(2)}) copy-start(f32[256]{0:T(256)S(1)} %broadcast_multiply_fusion) | copy-start | bytes 3076
  10.3 43.4 %copy-start.41 = (f32[256]{0:T(256)}, f32[256]{0:T(256)S(1)}, u32[]{:S(2)}) copy-start(f32[256]{0:T(256)S(1)} %fusion.111) | copy-start | bytes 3076
  11.0 42.7 %copy-start.34 = (f32[1536]{0:T(1024)}, f32[1536]{0:T(1024)S(1)}, u32[]{:S(2)}) copy-start(f32[1536]{0:T(1024)S(1)} %get-tuple-element.130) | copy-start | bytes 18436
  11.1 42.7 %copy-start.36 = (f32[1536]{0:T(1024)}, f32[1536]{0:T(1024)S(1)}, u32[]{:S(2)}) copy-start(f32[1536]{0:T(1024)S(1)} %get-tuple-element.128) | copy-start | bytes 18436
  13.4 21.5 %collective-permute-start = (bf16[1,1,256,1536]{3,2,1,0:T(8,128)(2,1)}, bf16[1,1,256,1536]{3,2,1,0:T(8,128)(2,1)S(1)}, u32[]{:S(2)}, u32[]{:S(2)}) collective-permute-start(bf16[1,1,256,1536]{3,2,1,0:T(8,128)(2,1)} %fusion.47), channel_id=1, source_target_pairs={{0,2},{1,3},{2,0},{3,1},{4,6},{5,7},{6,4},{7,5},{8,10},{9,11},{10,... | collective-permute-start | bytes 2359304 | tf_op jit(solution)/shard_map/ppermute | solution.py:162
  17.4 33.7 %collective-permute-start.7 = (bf16[1,1,256,1536]{3,2,1,0:T(8,128)(2,1)}, bf16[1,1,256,1536]{3,2,1,0:T(8,128)(2,1)}, u32[]{:S(2)}, u32[]{:S(2)}) collective-permute-start(bf16[1,1,256,1536]{3,2,1,0:T(8,128)(2,1)} %fusion.32), channel_id=1, source_target_pairs={{0,2},{1,3},{2,0},{3,1},{4,6},{5,7},{6,4},{7,5},{8,10},{9,11},{10,... | collective-permute-start | bytes 2359304 | tf_op jit(solution)/shard_map/ppermute | solution.py:162
  55.9 3.8 copy-start.17
  55.9 3.8 collective-permute-start.1
  58.6 14.2 %collective-permute-start.8 = (bf16[2,1,256,1536]{3,2,1,0:T(8,128)(2,1)S(1)}, bf16[2,1,256,1536]{3,2,1,0:T(8,128)(2,1)S(1)}, u32[]{:S(2)}, u32[]{:S(2)}) collective-permute-start(bf16[2,1,256,1536]{3,2,1,0:T(8,128)(2,1)S(1)} %pad_maximum_fusion.4), channel_id=1, source_target_pairs={{0,1},{1,0},{2,3},{3,2},{4,5},{5,4},{6,7},{7,6},{8,9},{9,8},{10,11... | collective-permute-start | bytes 4718600 | tf_op jit(solution)/shard_map/ppermute | solution.py:162
  61.6 5.7 copy-start.23
  67.3 6.0 copy-start.6
  73.3 10.4 %copy-start.25 = (bf16[2,2,256,1536]{3,2,1,0:T(8,128)(2,1)}, bf16[2,2,256,1536]{3,2,1,0:T(8,128)(2,1)S(1)}, u32[]{:S(2)}) copy-start(bf16[2,2,256,1536]{3,2,1,0:T(8,128)(2,1)S(1)} %pad_maximum_fusion.1) | copy-start | bytes 9437188
  83.7 3.7 copy-start.38
  84.4 3.1 collective-permute-start.2
  84.7 15.8 %copy-start.47 = (s32[1024]{0:T(1024)}, s32[1024]{0:T(1024)S(1)}, u32[]{:S(2)}) copy-start(s32[1024]{0:T(1024)S(1)} %fusion.98) | copy-start | bytes 12292
  88.5 8.7 %collective-permute-start.3 = (f32[512,128]{1,0:T(8,128)S(1)}, f32[512,128]{1,0:T(8,128)S(1)}, u32[]{:S(2)}, u32[]{:S(2)}) collective-permute-start(f32[512,128]{1,0:T(8,128)S(1)} %bitcast_add_fusion.1), channel_id=1, source_target_pairs={{0,2},{1,3},{2,0},{3,1},{4,6},{5,7},{6,4},{7,5},{8,10},{9,11},{10,... | collective-permute-start | bytes 786440 | tf_op jit(solution)/shard_map/ppermute | solution.py:162
  97.2 3.2 collective-permute-start.4
  100.4 3.1 copy-start.46
  100.4 7.6 %copy-start.32 = (bf16[512,128]{1,0:T(8,128)(2,1)}, bf16[512,128]{1,0:T(8,128)(2,1)S(1)}, u32[]{:S(2)}) copy-start(bf16[512,128]{1,0:T(8,128)(2,1)S(1)} %get-tuple-element.166) | copy-start | bytes 393220
  100.4 7.6 %copy-start.33 = (bf16[512,128]{1,0:T(8,128)(2,1)}, bf16[512,128]{1,0:T(8,128)(2,1)S(1)}, u32[]{:S(2)}) copy-start(bf16[512,128]{1,0:T(8,128)(2,1)S(1)} %get-tuple-element.167) | copy-start | bytes 393220
  121.7 3.8 copy-start.1
  152.4 3.8 copy-start.2
  156.2 52.6 %copy-start.11 = (f32[1024,768]{1,0:T(8,128)S(1)}, f32[1024,768]{1,0:T(8,128)}, u32[]{:S(2)}) copy-start(f32[1024,768]{1,0:T(8,128)} %compare_select_fusion.delta_ref) | copy-start | bytes 9437188
  208.8 3.8 copy-start.5
  212.5 87.4 %copy-start.14 = (bf16[1024,768]{1,0:T(8,128)(2,1)}, bf16[1024,768]{1,0:T(8,128)(2,1)S(1)}, u32[]{:S(2)}) copy-start(bf16[1024,768]{1,0:T(8,128)(2,1)S(1)} %get-tuple-element.136) | copy-start | bytes 4718596
  246.9 50.5 %copy-start.10 = (f32[1024,768]{1,0:T(8,128)S(1)}, f32[1024,768]{1,0:T(8,128)}, u32[]{:S(2)}) copy-start(f32[1024,768]{1,0:T(8,128)} %compare_select_fusion.1.delta_ref) | copy-start | bytes 9437188
  309.6 9.1 %copy-start.24 = (bf16[2,2,256,1536]{3,2,1,0:T(8,128)(2,1)S(1)}, bf16[2,2,256,1536]{3,2,1,0:T(8,128)(2,1)}, u32[]{:S(2)}) copy-start(bf16[2,2,256,1536]{3,2,1,0:T(8,128)(2,1)} %copy-done.23) | copy-start | bytes 9437188
  318.7 4.2 copy-start.55
  322.9 211.2 %reduce-scatter.5.cloned.1.call-start = ((), (), s32[]{:S(2)}) async-start(), calls=%async_computation.4 | async-start | bytes 2654208 | tf_op jit(solution)/shard_map/reduce_scatter | solution.py:324
  330.1 9.1 %collective-permute-start.9 = (f32[512,256]{1,0:T(8,128)}, f32[512,256]{1,0:T(8,128)}, u32[]{:S(2)}, u32[]{:S(2)}) collective-permute-start(f32[512,256]{1,0:T(8,128)} %bitcast.166), channel_id=1, source_target_pairs={{0,1},{1,0},{2,3},{3,2},{4,5},{5,4},{6,7},{7,6},{8,9},{9,8},{10,11... | collective-permute-start | bytes 1572872 | tf_op jit(solution)/shard_map/ppermute | solution.py:162
  333.6 8.5 %copy-start.26 = (bf16[2,2,256,1536]{3,2,1,0:T(8,128)(2,1)S(1)}, bf16[2,2,256,1536]{3,2,1,0:T(8,128)(2,1)}, u32[]{:S(2)}) copy-start(bf16[2,2,256,1536]{3,2,1,0:T(8,128)(2,1)} %copy-done.25) | copy-start | bytes 9437188
  333.6 8.5 %copy-start.51 = (bf16[1024,768]{1,0:T(8,128)(2,1)S(1)}, bf16[1024,768]{1,0:T(8,128)(2,1)}, u32[]{:S(2)}) copy-start(bf16[1024,768]{1,0:T(8,128)(2,1)} %get-tuple-element.140) | copy-start | bytes 4718596
  340.3 14.0 %collective-permute-start.10 = (f32[512,256]{1,0:T(8,128)S(1)}, f32[512,256]{1,0:T(8,128)}, u32[]{:S(2)}, u32[]{:S(2)}) collective-permute-start(f32[512,256]{1,0:T(8,128)S(1)} %bitcast_add_fusion), channel_id=1, source_target_pairs={{0,2},{1,3},{2,0},{3,1},{4,6},{5,7},{6,4},{7,5},{8,10},{9,11},{10,... | collective-permute-start | bytes 1572872 | tf_op jit(solution)/shard_map/ppermute | solution.py:162
  355.5 3.0 collective-permute-start.11
  356.4 4.8 copy-start.49
  361.3 4.6 copy-start.7
  377.6 76.5 %collective-permute-start.14 = (bf16[2,2,1,224,768]{4,3,2,1,0:T(8,128)(2,1)}, bf16[2,2,1,224,768]{4,3,2,1,0:T(8,128)(2,1)}, u32[]{:S(2)}, u32[]{:S(2)}) collective-permute-start(bf16[2,2,1,224,768]{4,3,2,1,0:T(8,128)(2,1)} %fusion.53), channel_id=1, source_target_pairs={{0,4},{4,0},{8,12},{12,8},{16,20},{20,16},{24,28},{28,24},{1,5},{5... | collective-permute-start | bytes 4128776 | tf_op jit(solution)/shard_map/ppermute | solution.py:162
  440.7 11.6 %all-to-all-start.1 = ((bf16[4,48,768]{2,1,0:T(8,128)(2,1)}), bf16[4,48,768]{2,1,0:T(8,128)(2,1)}, u32[]{:S(2)}, u32[]{:S(2)}) async-start(bf16[4,48,768]{2,1,0:T(8,128)(2,1)} %dynamic-slice_bitcast_fusion), calls=%async_computation.1 | async-start | bytes 589824 | tf_op jit(solution)/shard_map/all_to_all | solution.py:220
  444.8 173.6 %all-gather.3.cloned.1.call-start = ((), (), s32[]{:S(2)}) async-start(), calls=%async_computation.3 | async-start | bytes 2654208 | tf_op jit(solution)/shard_map/all_gather | solution.py:328
  454.2 3.2 copy-start.53
  454.2 3.7 copy-start.56
  456.1 29.8 %collective-permute-start.15 = (bf16[2,1,1,224,768]{4,3,2,1,0:T(8,128)(2,1)S(1)}, bf16[2,1,1,224,768]{4,3,2,1,0:T(8,128)(2,1)S(1)}, u32[]{:S(2)}, u32[]{:S(2)}) collective-permute-start(bf16[2,1,1,224,768]{4,3,2,1,0:T(8,128)(2,1)S(1)} %dynamic-slice_convert_fusion.2), channel_id=1, source_target_pairs={{0,8},{4,12},{8,0},{12,4},{16,24},{20,28},{24,16},{28,20},{1,9},{5... | collective-permute-start | bytes 2064392 | tf_op jit(solution)/shard_map/ppermute | solution.py:162
  462.4 23.6 %copy-start.28 = (bf16[1024,1536]{1,0:T(8,128)(2,1)}, bf16[1024,1536]{1,0:T(8,128)(2,1)S(1)}, u32[]{:S(2)}) copy-start(bf16[1024,1536]{1,0:T(8,128)(2,1)S(1)} %add_convert_fusion) | copy-start | bytes 9437188
  463.8 23.8 %copy-start.52 = (bf16[1024,768]{1,0:T(8,128)(2,1)S(1)}, bf16[1024,768]{1,0:T(8,128)(2,1)}, u32[]{:S(2)}) copy-start(bf16[1024,768]{1,0:T(8,128)(2,1)} %get-tuple-element.140) | copy-start | bytes 4718596
  463.8 51.6 %collective-permute-start.12 = (bf16[2,1,256,1536]{3,2,1,0:T(8,128)(2,1)}, bf16[2,1,256,1536]{3,2,1,0:T(8,128)(2,1)}, u32[]{:S(2)}, u32[]{:S(2)}) collective-permute-start(bf16[2,1,256,1536]{3,2,1,0:T(8,128)(2,1)} %constant_dynamic-slice_fusion.1), channel_id=1, source_target_pairs={{0,1},{1,0},{2,3},{3,2},{4,5},{5,4},{6,7},{7,6},{8,9},{9,8},{10,11... | collective-permute-start | bytes 4718600 | tf_op jit(solution)/shard_map/ppermute | solution.py:162
  486.0 18.4 %collective-permute-start.16 = (bf16[1,1,1,224,768]{4,3,2,1,0:T(8,128)(2,1)S(1)}, bf16[1,1,1,224,768]{4,3,2,1,0:T(8,128)(2,1)S(1)}, u32[]{:S(2)}, u32[]{:S(2)}) collective-permute-start(bf16[1,1,1,224,768]{4,3,2,1,0:T(8,128)(2,1)S(1)} %dynamic-slice_convert_fusion.3), channel_id=1, source_target_pairs={{0,16},{4,20},{8,24},{12,28},{16,0},{20,4},{24,8},{28,12},{1,17},{... | collective-permute-start | bytes 1032200 | tf_op jit(solution)/shard_map/ppermute | solution.py:162
  492.1 12.4 %copy-start.27 = (bf16[1024,1536]{1,0:T(8,128)(2,1)}, bf16[1024,1536]{1,0:T(8,128)(2,1)S(1)}, u32[]{:S(2)}) copy-start(bf16[1024,1536]{1,0:T(8,128)(2,1)S(1)} %convolution_convert_fusion) | copy-start | bytes 9437188
  493.5 40.7 %collective-permute-start.5 = (bf16[2,1,256,1536]{3,2,1,0:T(8,128)(2,1)}, bf16[2,1,256,1536]{3,2,1,0:T(8,128)(2,1)}, u32[]{:S(2)}, u32[]{:S(2)}) collective-permute-start(bf16[2,1,256,1536]{3,2,1,0:T(8,128)(2,1)} %constant_dynamic-slice_fusion.4), channel_id=1, source_target_pairs={{0,1},{1,0},{2,3},{3,2},{4,5},{5,4},{6,7},{7,6},{8,9},{9,8},{10,11... | collective-permute-start | bytes 4718600 | tf_op jit(solution)/shard_map/ppermute | solution.py:162
  505.2 9.8 %all-to-all-start = ((bf16[4,48,768]{2,1,0:T(8,128)(2,1)}), bf16[4,48,768]{2,1,0:T(8,128)(2,1)S(1)}, u32[]{:S(2)}, u32[]{:S(2)}) async-start(bf16[4,48,768]{2,1,0:T(8,128)(2,1)} %bitcast.25), calls=%async_computation | async-start | bytes 589824 | tf_op jit(solution)/shard_map/all_to_all | solution.py:220
  508.7 145.2 %all-gather.5.cloned.1.call-start = ((), (), s32[]{:S(2)}) async-start(), calls=%async_computation.5 | async-start | bytes 2654208 | tf_op jit(solution)/shard_map/all_gather | solution.py:325
  515.3 17.8 %collective-permute-start.17 = (bf16[1,1,1,224,768]{4,3,2,1,0:T(8,128)(2,1)S(1)}, bf16[1,1,1,224,768]{4,3,2,1,0:T(8,128)(2,1)S(1)}, u32[]{:S(2)}, u32[]{:S(2)}) collective-permute-start(bf16[1,1,1,224,768]{4,3,2,1,0:T(8,128)(2,1)S(1)} %maximum_bitcast_fusion), channel_id=1, source_target_pairs={{0,16},{4,20},{8,24},{12,28},{16,0},{20,4},{24,8},{28,12},{1,17},{... | collective-permute-start | bytes 1032200 | tf_op jit(solution)/shard_map/ppermute | solution.py:162
  519.5 44.5 %collective-permute-start.13 = (bf16[1,1,256,1536]{3,2,1,0:T(8,128)(2,1)S(1)}, bf16[1,1,256,1536]{3,2,1,0:T(8,128)(2,1)S(1)}, u32[]{:S(2)}, u32[]{:S(2)}) collective-permute-start(bf16[1,1,256,1536]{3,2,1,0:T(8,128)(2,1)S(1)} %dynamic-slice_convert_fusion), channel_id=1, source_target_pairs={{0,2},{1,3},{2,0},{3,1},{4,6},{5,7},{6,4},{7,5},{8,10},{9,11},{10,... | collective-permute-start | bytes 2359304 | tf_op jit(solution)/shard_map/ppermute | solution.py:162
  534.1 27.1 %collective-permute-start.18 = (bf16[2,1,1,224,768]{4,3,2,1,0:T(8,128)(2,1)}, bf16[2,1,1,224,768]{4,3,2,1,0:T(8,128)(2,1)}, u32[]{:S(2)}, u32[]{:S(2)}) collective-permute-start(bf16[2,1,1,224,768]{4,3,2,1,0:T(8,128)(2,1)} %pad_maximum_fusion.6), channel_id=1, source_target_pairs={{0,8},{4,12},{8,0},{12,4},{16,24},{20,28},{24,16},{28,20},{1,9},{5... | collective-permute-start | bytes 2064392 | tf_op jit(solution)/shard_map/ppermute | solution.py:162
  536.8 27.3 %copy-start.9 = (bf16[1,256,1536]{2,1,0:T(8,128)(2,1)S(1)}, bf16[1,256,1536]{2,1,0:T(8,128)(2,1)}, u32[]{:S(2)}) copy-start(bf16[1,256,1536]{2,1,0:T(8,128)(2,1)} %param.13) | copy-start | bytes 2359300
  536.8 27.3 %copy-start.13 = (f32[2,1,256,1536]{3,2,1,0:T(8,128)S(1)}, f32[2,1,256,1536]{3,2,1,0:T(8,128)}, u32[]{:S(2)}) copy-start(f32[2,1,256,1536]{3,2,1,0:T(8,128)} %copy-done.12) | copy-start | bytes 9437188
  536.8 27.3 %copy-start.35 = (f32[1536]{0:T(1024)S(1)}, f32[1536]{0:T(1024)}, u32[]{:S(2)}) copy-start(f32[1536]{0:T(1024)} %copy-done.34) | copy-start | bytes 18436
  536.8 27.3 %copy-start.40 = (f32[256]{0:T(256)S(1)}, f32[256]{0:T(256)}, u32[]{:S(2)}) copy-start(f32[256]{0:T(256)} %copy-done.39) | copy-start | bytes 3076
  536.8 28.4 %collective-permute-start.6 = (bf16[1,1,256,1536]{3,2,1,0:T(8,128)(2,1)S(1)}, bf16[1,1,256,1536]{3,2,1,0:T(8,128)(2,1)S(1)}, u32[]{:S(2)}, u32[]{:S(2)}) collective-permute-start(bf16[1,1,256,1536]{3,2,1,0:T(8,128)(2,1)S(1)} %dynamic-slice_convert_fusion.1), channel_id=1, source_target_pairs={{0,2},{1,3},{2,0},{3,1},{4,6},{5,7},{6,4},{7,5},{8,10},{9,11},{10,... | collective-permute-start | bytes 2359304 | tf_op jit(solution)/shard_map/ppermute | solution.py:162
  562.6 43.8 %collective-permute-start.19 = (bf16[2,2,1,224,768]{4,3,2,1,0:T(8,128)(2,1)S(1)}, bf16[2,2,1,224,768]{4,3,2,1,0:T(8,128)(2,1)S(1)}, u32[]{:S(2)}, u32[]{:S(2)}) collective-permute-start(bf16[2,2,1,224,768]{4,3,2,1,0:T(8,128)(2,1)S(1)} %pad_maximum_fusion.5), channel_id=1, source_target_pairs={{0,4},{4,0},{8,12},{12,8},{16,20},{20,16},{24,28},{28,24},{1,5},{5... | collective-permute-start | bytes 4128776 | tf_op jit(solution)/shard_map/ppermute | solution.py:162
  623.7 4.4 copy-start.15
  (19 other events, 36.2 us)
Sparse Core Ops, SparseCore 0:
  323.0 115.2 all-reduce.5
  442.2 78.1 reduce-scatter.4
  522.9 78.1 all-gather.2
  603.3 50.5 all-gather.4

commit v2 on v1

v2 whole, which is shorter than its diff:
```python
import jax
import jax.numpy as jnp
from jax import lax
from jax.experimental import pallas as pl
from jax.experimental.pallas import tpu as pltpu
from jax.sharding import PartitionSpec as P

epsilon = 1e-06
f32, bf16 = jnp.float32, jnp.bfloat16
LOG2E = 1.4426950408889634
N = 16
CH = 16
TB = 128
GROUP = 4


def dot(a, b):
    return lax.dot_general(a, b, (((1,), (0,)), ((), ())), preferred_element_type=f32)


def dot_t(a, b):
    return lax.dot_general(a, b, (((1,), (1,)), ((), ())), preferred_element_type=f32)


def contract_rows(left, right):
    return lax.dot_general(left, right, (((0,), (0,)), ((), ())), preferred_element_type=f32)


def tiles(width):
    return [slice(lo, lo + 128) for lo in range(0, width, 128)]


def across(row):
    return jnp.broadcast_to(row, (N, row.shape[1]))


def along(column):
    return jnp.broadcast_to(column, (N, 128))


def tree(values):
    while len(values) > 1:
        values = [a + b for a, b in zip(values[::2], values[1::2])] + values[len(values) & ~1 :]
    return values[0]


def places(shape, dim):
    return lax.broadcasted_iota(jnp.int32, shape, dim)


def spread(p, first):
    shape = (p.shape[1], CH * N)
    choose = (places(shape, 0) == first + places(shape, 1) % N).astype(bf16)
    shape = (p.shape[0], CH * N)
    keep = places(shape, 1) // N == places(shape, 0) % CH
    return jnp.where(keep, dot(p, choose), 0.0).astype(bf16)


def turned(p, first):
    shape = (N, p.shape[1])
    choose = (places(shape, 1) == first + places(shape, 0)).astype(bf16)
    return dot_t(choose, p)


def group_columns(mat, group):
    return pltpu.roll(mat, (TB - group * GROUP * CH) % TB, 1)


def work(steps):
    return pl.CostEstimate(flops=100 * steps, bytes_accessed=steps // 4, transcendentals=0)


def scan_kernel(p_ref, u_ref, wdt_ref, bdt_ref, a_ref, y_ref, s_ref, delta_ref, du_scr, cd_scr, state_scr):
    lanes = tiles(delta_ref.shape[1])
    rank = p_ref.shape[1] - 2 * N

    @pl.when(pl.program_id(0) == 0)
    def _():
        state_scr[...] = jnp.zeros_like(state_scr)

    p = p_ref[...]
    pre = dot_t(p, wdt_ref[...]) + bdt_ref[...]
    delta = jnp.maximum(pre, 0.0) + jnp.log1p(jnp.exp(-jnp.abs(pre)))
    delta_ref[...] = delta
    du_scr[...] = delta * u_ref[...].astype(f32)
    cd_scr[...] = spread(p, rank + N)
    b_turned = turned(p, rank)
    s_ref[0, 0:N, :] = state_scr[...].astype(bf16)

    def group(step, state):
        b_all = group_columns(b_turned, step)
        state = list(state)
        for j in range(GROUP):
            base = pl.multiple_of((step * GROUP + j) * CH, CH)
            rows = pl.ds(base, CH)
            d_view = delta_ref.at[rows, :]
            du_view = du_scr.at[rows, :]
            s_view = s_ref.at[0, pl.ds(pl.multiple_of(base * N + N, N), CH * N), :]
            for t in range(CH):
                b = along(b_all[:, j * CH + t : j * CH + t + 1])
                for i, ls in enumerate(lanes):
                    decay = jnp.exp2(across(d_view[t : t + 1, ls]) * a_ref[:, ls])
                    state[i] = decay * state[i] + across(du_view[t : t + 1, ls]) * b
                    s_view[t * N : (t + 1) * N, ls] = state[i].astype(bf16)
            y_ref[rows, :] = dot(cd_scr[rows, :], s_view[...]).astype(y_ref.dtype)
        return tuple(state)

    state = lax.fori_loop(0, TB // CH // GROUP, group, tuple(state_scr[:, ls] for ls in lanes))
    for i, ls in enumerate(lanes):
        state_scr[:, ls] = state[i]


def scan_forward(p, u, wdt, bdt, a_two, y_dtype):
    total, chans = u.shape
    blocks = total // TB
    rows = lambda i: (i, 0)
    whole = lambda i: (0, 0)
    wide = pl.BlockSpec((TB, chans), rows)
    return pl.pallas_call(
        scan_kernel,
        grid=(blocks,),
        in_specs=[
            pl.BlockSpec((TB, p.shape[1]), rows),
            wide,
            pl.BlockSpec(wdt.shape, whole),
            pl.BlockSpec((1, chans), whole),
            pl.BlockSpec((N, chans), whole),
        ],
        out_specs=[wide, pl.BlockSpec((1, (TB + 1) * N, chans), lambda i: (i, 0, 0)), wide],
        out_shape=[
            jax.ShapeDtypeStruct((total, chans), y_dtype),
            jax.ShapeDtypeStruct((blocks, (TB + 1) * N, chans), bf16),
            jax.ShapeDtypeStruct((total, chans), f32),
        ],
        scratch_shapes=[
            pltpu.VMEM((TB, chans), f32),
            pltpu.VMEM((TB, CH * N), bf16),
            pltpu.VMEM((N, chans), f32),
        ],
        compiler_params=pltpu.CompilerParams(vmem_limit_bytes=40 << 20),
        cost_estimate=work(20 * total * chans * N),
        name="scan_out",
    )(p, u, wdt, bdt, a_two)


def lane_sums(part):
    sums = dot_t(jnp.ones((16, 128), bf16), part)[0:8]
    own = places((8, 128), 1) // N == places((8, 128), 0)
    rows = []
    for lo in range(0, part.shape[0], 128):
        held = jnp.where(own, sums[:, lo : lo + 128], 0.0)
        for shift in (64, 32, 16):
            held = held + pltpu.roll(held, shift, 1)
        rows.append(held)
    return jnp.concatenate(rows, axis=0)


def adjoint_kernel(
    p_ref, delta_ref, u_ref, g_ref, wdt_ref, a_ref, alow_ref, s_ref,
    du_ref, dp_ref, gw_ref, gb_ref, da_ref,
    dux, bd_scr, dd_scr, lam, ra, pb, pc, carry,
):
    lanes = tiles(delta_ref.shape[1])
    rank = p_ref.shape[1] - 2 * N

    @pl.when(pl.program_id(0) == 0)
    def _():
        for ref in (carry, da_ref, gw_ref, gb_ref):
            ref[...] = jnp.zeros_like(ref)

    p = p_ref[...]
    dux[...] = delta_ref[...] * u_ref[...].astype(f32)
    bd_scr[...] = spread(p, rank)
    c_turned = turned(p, rank + N)
    adder = (places((CH, CH * N), 1) // N == places((CH, CH * N), 0)).astype(bf16)

    def back(base, j, c_cols, held):
        d_view = delta_ref.at[pl.ds(base, CH), :]
        g_view = g_ref.at[pl.ds(base, CH), :]
        du_view = dux.at[pl.ds(base, CH), :]
        before = s_ref.at[0, pl.ds(pl.multiple_of(base * N, N), (CH + 1) * N), :]
        states = pl.ds(pl.multiple_of(base * N, CH * N), CH * N)
        pb_view, pc_view = pb.at[states, :], pc.at[states, :]
        held, pair, total = list(held), [None] * len(lanes), [None] * len(lanes)
        for t in reversed(range(CH)):
            rs = slice(t * N, (t + 1) * N)
            after = slice((t + 1) * N, (t + 2) * N)
            c = along(c_cols[:, t : t + 1])
            sum_b, sum_c = [], []
            for i, ls in enumerate(lanes):
                d = across(d_view[t : t + 1, ls])
                g = across(g_view[t : t + 1, ls]).astype(f32)
                grad = held[i] + g * c
                held[i] = jnp.exp2(d * a_ref[:, ls]) * grad
                lam[j, rs, ls] = grad.astype(bf16)
                r = held[i].astype(bf16) * before[rs, ls]
                ra[j, rs, ls] = r * alow_ref[:, ls]
                rd = r * d.astype(bf16)
                if t % 2:
                    pair[i] = rd
                else:
                    both = (pair[i] + rd).astype(f32)
                    total[i] = both if total[i] is None else total[i] + both
                sum_b.append(grad * across(du_view[t : t + 1, ls]))
                sum_c.append(before[after, ls] * g.astype(bf16))
            pb_view[rs, :] = tree(sum_b).astype(bf16)
            pc_view[rs, :] = tree(sum_c).astype(bf16)
        for i, ls in enumerate(lanes):
            da_ref[:, ls] += total[i]
        return tuple(held)

    def sums(base, j):
        rows = pl.ds(base, CH)
        d_in = dot(bd_scr[rows, :], lam[j])
        d_exp = dot(adder, ra[j])
        dd_scr[rows, :] = d_exp + u_ref[rows, :].astype(f32) * d_in
        du_ref[rows, :] = (delta_ref[rows, :] * d_in).astype(du_ref.dtype)

    def group(step, held):
        place = TB // CH // GROUP - 1 - step
        c_all = group_columns(c_turned, place)
        for j in reversed(range(GROUP)):
            base = pl.multiple_of((place * GROUP + j) * CH, CH)
            held = back(base, j, c_all[:, j * CH : (j + 1) * CH], held)
            sums(base, j)
        return held

    held = lax.fori_loop(0, TB // CH // GROUP, group, tuple(carry[:, ls] for ls in lanes))
    for i, ls in enumerate(lanes):
        carry[:, ls] = held[i]
    delta = delta_ref[...]
    slope = jnp.where(
        delta < 0.01, delta * (1.0 - delta * (0.5 - delta * (1.0 / 6.0))), 1.0 - jnp.exp(-delta)
    )
    d_pre = dd_scr[...] * slope
    gb_ref[...] += jnp.sum(d_pre, axis=0, keepdims=True)
    d_pre = d_pre.astype(bf16)
    gw_ref[...] += contract_rows(d_pre, p)
    d_low = dot(d_pre, wdt_ref[...])
    lane = places(d_low.shape, 1)
    tail = jnp.where(lane < rank + N, lane_sums(pb[...]), lane_sums(pc[...]))
    dp_ref[...] = jnp.where(lane < rank, d_low, tail)


def scan_adjoint(p, delta, u, g, wdt, a_two, a_low, states, du_dtype):
    total, chans = delta.shape
    blocks = total // TB
    rows = lambda i: (blocks - 1 - i, 0)
    first = lambda i: (blocks - 1 - i, 0, 0)
    whole = lambda i: (0, 0)
    wide = pl.BlockSpec((TB, chans), rows)
    narrow = pl.BlockSpec((TB, p.shape[1]), rows)
    per_state = pl.BlockSpec((N, chans), whole)
    return pl.pallas_call(
        adjoint_kernel,
        grid=(blocks,),
        in_specs=[
            narrow,
            wide,
            wide,
            wide,
            pl.BlockSpec(wdt.shape, whole),
            per_state,
            per_state,
            pl.BlockSpec((1, (TB + 1) * N, chans), first),
        ],
        out_specs=[
            wide,
            narrow,
            pl.BlockSpec(wdt.shape, whole),
            pl.BlockSpec((1, chans), whole),
            per_state,
        ],
        out_shape=[
            jax.ShapeDtypeStruct((total, chans), du_dtype),
            jax.ShapeDtypeStruct(p.shape, f32),
            jax.ShapeDtypeStruct(wdt.shape, f32),
            jax.ShapeDtypeStruct((1, chans), f32),
            jax.ShapeDtypeStruct((N, chans), f32),
        ],
        scratch_shapes=[
            pltpu.VMEM((TB, chans), f32),
            pltpu.VMEM((TB, CH * N), bf16),
            pltpu.VMEM((TB, chans), f32),
            pltpu.VMEM((GROUP, CH * N, chans), bf16),
            pltpu.VMEM((GROUP, CH * N, chans), bf16),
            pltpu.VMEM((TB * N, 128), bf16),
            pltpu.VMEM((TB * N, 128), bf16),
            pltpu.VMEM((N, chans), f32),
        ],
        compiler_params=pltpu.CompilerParams(vmem_limit_bytes=48 << 20),
        cost_estimate=work(40 * total * chans * N),
        name="scan_back",
    )(p, delta, u, g, wdt, a_two, a_low, states)


def silu_slope(value):
    sigmoid = jax.nn.sigmoid(value)
    return sigmoid * (1.0 + value * (1.0 - sigmoid))


def normalize(rows_in, shift, scale):
    mean = jnp.mean(rows_in, axis=-1, keepdims=True)
    centered = rows_in - mean
    variance = jnp.mean(centered * centered, axis=-1, keepdims=True)
    return centered * lax.rsqrt(variance + epsilon) * (1.0 + scale) + shift


def partner(block, axis, bit):
    return lax.ppermute(block, axis, [(i, i ^ bit) for i in range(lax.axis_size(axis))])


def bits_down(axis):
    bit = lax.axis_size(axis) // 2
    while bit:
        yield bit
        bit //= 2


def bits_up(axis):
    return reversed(list(bits_down(axis)))


def gather_rows(block, axis, bits):
    index = lax.axis_index(axis)
    size = lax.axis_size(axis)
    held = block[(None,) * len(bits)]
    places = [b.bit_length() - 1 for b in bits]
    for bit, place in zip(bits, places):
        other = partner(held, axis, bit)
        dim = len(bits) - 1 - place
        upper = (index & bit) != 0
        held = jnp.concatenate([jnp.where(upper, other, held), jnp.where(upper, held, other)], axis=dim)
    return held.reshape((size,) + block.shape)


def split_bits(blocks, bits):
    return blocks.reshape((2,) * len(bits) + blocks.shape[1:])


def scatter_hop(held, axis, bits, hop):
    bit = bits[hop]
    dim = len(bits) - 1 - (bit.bit_length() - 1)
    mine = (lax.axis_index(axis) & bit) // bit
    keep = lax.dynamic_index_in_dim(held, mine, dim, keepdims=True)
    send = lax.dynamic_index_in_dim(held, 1 - mine, dim, keepdims=True).astype(bf16)
    return keep.astype(f32) + partner(send, axis, bit).astype(f32)


def scatter_sum(blocks, axis, bits):
    held = split_bits(blocks, bits)
    for hop in range(len(bits)):
        held = scatter_hop(held, axis, bits, hop)
    return held.reshape(blocks.shape[1:])


def sum_seq(value):
    index = lax.axis_index("seq")
    rows = value.shape[0] // 2
    halves = value.reshape((2, rows) + value.shape[1:])
    mine = index & 1
    held = lax.dynamic_index_in_dim(halves, mine, 0, keepdims=False) + partner(
        lax.dynamic_index_in_dim(halves, 1 - mine, 0, keepdims=False), "seq", 1
    )
    bit = 2
    while bit < lax.axis_size("seq"):
        held = held + partner(held, "seq", bit)
        bit *= 2
    other = partner(held, "seq", 1)
    upper = mine != 0
    return jnp.concatenate([jnp.where(upper, other, held), jnp.where(upper, held, other)], axis=0)


def sum_pair(first, second):
    odd = (lax.axis_index("seq") & 1) != 0
    held = jnp.where(odd, second, first) + partner(jnp.where(odd, first, second), "seq", 1)
    bit = 2
    while bit < lax.axis_size("seq"):
        held = held + partner(held, "seq", bit)
        bit *= 2
    other = partner(held, "seq", 1)
    return jnp.where(odd, other, held), jnp.where(odd, held, other)


def across_seq(blocks):
    return lax.all_to_all(blocks, "seq", split_axis=0, concat_axis=0, tiled=True)


def join_out(early, rows_each, chans):
    owners, _, strip = early.shape
    sides = rows_each * owners // chans
    rows = chans // owners

    def kernel(in_ref, out_ref):
        for k in range(sides):
            out_ref[:, k * strip : (k + 1) * strip] = in_ref[0, k * rows : (k + 1) * rows, :].astype(f32)

    if rows % 16:
        blocks = early[:, :rows_each].reshape(owners, sides, rows, strip).swapaxes(1, 2)
        return blocks.reshape(chans, sides * strip).astype(f32)
    return pl.pallas_call(
        kernel,
        grid=(owners,),
        in_specs=[pl.BlockSpec((1, rows_each, strip), lambda i: (i, 0, 0))],
        out_specs=pl.BlockSpec((rows, sides * strip), lambda i: (i, 0)),
        out_shape=jax.ShapeDtypeStruct((chans, sides * strip), f32),
        cost_estimate=pl.CostEstimate(flops=0, bytes_accessed=24 << 20, transcendentals=0),
        name="join_out",
    )(early)


def join_gate(early, rows_each, inner, parts):
    owners, _, chans = early.shape
    rows = rows_each // parts

    def kernel(in_ref, out_ref):
        for k in range(parts):
            out_ref[:, k * chans : (k + 1) * chans] = in_ref[0, k * rows : (k + 1) * rows, :].astype(f32)

    if rows % 16:
        blocks = early[:, rows_each:].reshape(owners, parts, rows, chans).swapaxes(1, 2)
        return blocks.reshape(owners * rows, inner).astype(f32)
    return pl.pallas_call(
        kernel,
        grid=(owners,),
        in_specs=[pl.BlockSpec((1, rows_each, chans), lambda i: (i, 1, 0))],
        out_specs=pl.BlockSpec((rows, inner), lambda i: (i, 1)),
        out_shape=jax.ShapeDtypeStruct((owners * rows, 2 * inner), f32),
        cost_estimate=pl.CostEstimate(flops=0, bytes_accessed=24 << 20, transcendentals=0),
        name="join_gate",
    )(early)


def join_in(gate_half, left, right, parts):
    owners, rows_each, half = left.shape
    rows = rows_each // parts

    def kernel(left_ref, right_ref, _, out_ref):
        for k in range(parts):
            for side, ref in enumerate((left_ref, right_ref)):
                lo = (2 * k + side) * half
                out_ref[:, lo : lo + half] = ref[0, k * rows : (k + 1) * rows, :].astype(f32)

    if rows % 16:
        both = jnp.concatenate([left, right[:, :rows_each]], axis=2)
        both = both.reshape(owners, parts, rows, 2 * half).swapaxes(1, 2).reshape(owners * rows, -1)
        return jnp.concatenate([both.astype(f32), gate_half], axis=1)
    block = pl.BlockSpec((1, rows_each, half), lambda i: (i, 0, 0))
    return pl.pallas_call(
        kernel,
        grid=(owners,),
        in_specs=[block, block, pl.BlockSpec(memory_space=pl.ANY)],
        out_specs=pl.BlockSpec((rows, 2 * half * parts), lambda i: (i, 0)),
        out_shape=jax.ShapeDtypeStruct(gate_half.shape, f32),
        input_output_aliases={2: 0},
        cost_estimate=pl.CostEstimate(flops=0, bytes_accessed=24 << 20, transcendentals=0),
        name="join_in",
    )(left, right, gate_half)


def shards(
    tokens,
    modulation,
    heights,
    w_in,
    w_x,
    w_dt,
    b_dt,
    a_log,
    d_skip,
    conv_w,
    conv_b,
    w_out,
    cotangent,
):
    _, seq_len, width = tokens.shape
    parts = lax.axis_size("seq")
    data_parts = lax.axis_size("dp")
    inner = w_out.shape[0]
    chans = inner // parts
    rank = w_dt.shape[1]
    taps = conv_w.shape[1]
    total = seq_len * parts
    part = lax.axis_index("seq")
    seq_down, seq_up = list(bits_down("seq")), list(bits_up("seq"))
    dp_down, dp_up = list(bits_down("dp")), list(bits_up("dp"))

    def own(array, axis=0, offset=0):
        return lax.dynamic_slice_in_dim(array, offset + part * chans, chans, axis)

    w_conv_in, w_gate_in = own(w_in, 1), own(w_in, 1, inner)
    wx, wdt, bdt, wout = own(w_x), own(w_dt), own(b_dt)[None], own(w_out)
    wdt = jnp.pad(wdt, ((0, 0), (0, 2 * N)))
    dsk, cw, cb = own(d_skip), own(conv_w), own(conv_b)
    a_state = -jnp.exp(own(a_log).T)
    a_two = a_state * LOG2E
    a_low = a_state.astype(bf16)
    shift, scale, gate = modulation[0, 0:1], modulation[0, 1:2], modulation[0, 2:3]

    x_own = tokens[0].astype(f32)
    normed, norm_back = jax.vjp(lambda rows_in: normalize(rows_in, shift, scale), x_own)
    hmod = gather_rows(normed.astype(bf16), "seq", seq_down).reshape(total, width)
    d_res = cotangent[0].astype(f32)

    x_conv = dot(hmod, w_conv_in).astype(bf16)
    z_gate = dot(hmod, w_gate_in)
    padded = jnp.concatenate([jnp.zeros((taps - 1, chans), bf16), x_conv], axis=0).astype(f32)
    pre_conv = cb + sum(padded[k : k + total] * cw[:, k] for k in range(taps))
    u_low = jax.nn.silu(pre_conv).astype(bf16)
    proj = sum_seq(dot(u_low, wx)).astype(bf16)

    height = heights[0]
    wide = total // height
    column = total - 1 - jnp.arange(total, dtype=jnp.int32)
    order = column % height * wide + column // height
    to_columns = (order[:, None] == jnp.arange(total, dtype=jnp.int32)[None, :]).astype(bf16)

    def columns_of(value):
        return dot(to_columns, value).astype(bf16)

    def rows_of(value):
        return contract_rows(to_columns, value)

    u_col = columns_of(u_low)
    proj_col = columns_of(proj)

    proj, d_branch = lax.optimization_barrier((proj, (gate * d_res).astype(bf16)))
    d_branch = gather_rows(d_branch, "seq", seq_down)
    y_fwd, s_row, delta_row = scan_forward(proj, u_low, wdt, bdt, a_two, f32)
    y_col, s_col, delta_col = scan_forward(proj_col, u_col, wdt, bdt, a_two, bf16)
    y_fwd, d_branch = lax.optimization_barrier((y_fwd, d_branch))
    d_branch = d_branch.reshape(total, width)
    u_full = u_low.astype(f32)
    y_all = y_fwd + rows_of(y_col) + dsk * u_full
    silu_z = jax.nn.silu(z_gate)
    gated = (y_all * silu_z).astype(bf16)
    d_gated = dot_t(d_branch, wout)
    d_y = d_gated * silu_z
    d_z = (d_gated * y_all * silu_slope(z_gate)).astype(bf16)
    g_dskip = jnp.sum(d_y * u_full, axis=0)
    rows_each = width // data_parts
    sides = width // chans

    def by_owner(grad):
        return grad.reshape(parts, data_parts, -1, grad.shape[1]).swapaxes(0, 1).reshape(data_parts, rows_each, -1)

    strips = [d_branch[:, k * chans : (k + 1) * chans] for k in range(sides)]
    payload = jnp.concatenate(
        [contract_rows(gated, strip).astype(bf16).reshape(data_parts, -1, chans) for strip in strips]
        + [by_owner(contract_rows(hmod, d_z).astype(bf16))],
        axis=1,
    )
    payload, d_y = lax.optimization_barrier((payload, d_y))
    early = lax.psum_scatter(payload, "dp", scatter_dimension=0, tiled=True)[0]

    dy_col = columns_of(d_y.astype(bf16))
    du_row, p_row, gw_row, gb_row, da_row = scan_adjoint(
        proj, delta_row, u_low, d_y, wdt, a_two, a_low, s_row, f32
    )
    du_col, p_col, gw_col, gb_col, da_col = scan_adjoint(
        proj_col, delta_col, u_col, dy_col, wdt, a_two, a_low, s_col, bf16
    )
    early, p_row, p_col = lax.optimization_barrier((early, p_row, p_col))
    mine = across_seq(early[rows_each:].reshape(parts, -1, chans)).reshape(rows_each, chans)
    mine, p_row, p_col = lax.optimization_barrier((mine, p_row, p_col))
    early = lax.all_gather(jnp.concatenate([early[:rows_each], mine], axis=0), "dp", axis=0)
    p_row, p_col = sum_pair(p_row, p_col)
    d_proj = (p_row + rows_of(p_col.astype(bf16))).astype(bf16)
    g_wx = contract_rows(u_low, d_proj)
    d_u = du_row + rows_of(du_col) + d_y * dsk + dot_t(d_proj, wx)
    d_pre_conv = d_u * silu_slope(pre_conv)
    g_convb = jnp.sum(d_pre_conv, axis=0)
    g_convw = jnp.stack([jnp.sum(padded[k : k + total] * d_pre_conv, axis=0) for k in range(taps)])
    later = jnp.concatenate([d_pre_conv, jnp.zeros((taps - 1, chans), f32)], axis=0)
    d_xconv = sum(cw[:, k] * later[taps - 1 - k : taps - 1 - k + total] for k in range(taps)).astype(bf16)

    half = chans // 2
    singles = [(da_row + da_col) * a_state, gb_row + gb_col, g_dskip[None], g_convb[None], g_convw]
    singles = jnp.concatenate(singles, axis=0).astype(bf16)
    count = singles.shape[0]
    lane = jnp.arange(wdt.shape[1])[None, :]
    singles = contract_rows(singles, (lane == rank + jnp.arange(count)[:, None]).astype(bf16))
    small = jnp.concatenate([g_wx, jnp.where(lane < rank, gw_row + gw_col, singles)], axis=1).astype(bf16)
    columns = small.shape[1]
    if columns <= half:
        small = jnp.pad(small, ((0, 0), (0, half - columns)))
    small = small.reshape(data_parts, -1, half)

    def to_owner(held):
        held = held.astype(bf16)
        mine = across_seq(held[:rows_each].reshape(parts, -1, half)).reshape(rows_each, half)
        return jnp.concatenate([mine, held[rows_each:]], axis=0)

    left = by_owner(contract_rows(hmod, d_xconv[:, :half]).astype(bf16))
    right = by_owner(contract_rows(hmod, d_xconv[:, half:]).astype(bf16))
    right = jnp.concatenate([right, small], axis=1)
    left, right, early = lax.optimization_barrier((left, right, early))
    other_way = dp_up[1:] + dp_up[:1]
    left = scatter_hop(split_bits(left, dp_up), "dp", dp_up, 0)
    right = scatter_hop(split_bits(right, dp_up), "dp", other_way, 0)
    g_out = join_out(early, rows_each, chans)
    g_gate = join_gate(early, rows_each, inner, parts)
    left, right, g_out, g_gate = lax.optimization_barrier((left, right, g_out, g_gate))
    for hop in range(1, len(dp_up)):
        left = scatter_hop(left, "dp", dp_up, hop)
        right = scatter_hop(right, "dp", other_way, hop)
    left = to_owner(left.reshape(rows_each, half))
    right = to_owner(right.reshape(-1, half))
    left = gather_rows(left, "dp", dp_down)
    right = gather_rows(right, "dp", other_way[::-1])
    small = right[:, rows_each:].reshape(-1, half) if columns <= half else right[:, rows_each:].reshape(chans, -1)
    small = small.astype(f32)
    g_in = join_in(g_gate, left, right, parts)

    branch = scatter_sum(dot(gated, wout).astype(bf16).reshape(parts, seq_len, width), "seq", seq_up)
    result = (x_own + gate * branch).astype(bf16)

    d_h = dot_t(d_xconv, w_conv_in) + dot_t(d_z, w_gate_in)
    d_h = scatter_sum(d_h.astype(bf16).reshape(parts, seq_len, width), "seq", seq_up)
    d_x = d_res + norm_back(d_h)[0]

    edges = [0]
    for size in (w_x.shape[1], rank, N, 1, 1, 1, taps):
        edges.append(edges[-1] + size)
    pieces = [small[:, lo:hi] for lo, hi in zip(edges, edges[1:])]
    return (
        result[None],
        d_x[None],
        g_in,
        pieces[0],
        pieces[1],
        pieces[3][:, 0],
        pieces[2],
        pieces[4][:, 0],
        pieces[6],
        pieces[5][:, 0],
        g_out,
    )


def solution(mesh):
    placed = (
        P("dp", "seq", None),
        P("dp", None, None),
        P("dp"),
        P(),
        P(),
        P(),
        P(),
        P(),
        P(),
        P(),
        P(),
        P(),
        P("dp", "seq", None),
    )
    return jax.shard_map(
        shards,
        mesh=mesh,
        in_specs=placed,
        out_specs=(
            P("dp", "seq", None),
            P("dp", "seq", None),
            P("seq", None),
            P("seq", None),
            P("seq", None),
            P("seq"),
            P("seq", None),
            P("seq"),
            P("seq", None),
            P("seq"),
            P("seq", None),
        ),
        check_vma=False,
    )
```

time: 674 us -> 491 us (0.73)
  waiting for transfers between devices: 234 us -> 130 us
  matrix products: 98.9 us -> 57.5 us
  local copies, waits for them, and re-layouts: 80.9 us -> 41 us
  blocking collectives: 0 us -> 8.91 us
  other arithmetic: 57.7 us -> 49.4 us
    unnamed x5 -> x2, waiting for transfers between devices: 58.4 us -> 0.03 us
    ppermute x20 -> x26, waiting for transfers between devices: 151 us -> 103 us  [partner(): lax.ppermute(block, axis, [(i, i ^ bit) for i in range(lax.axis_size(axis...]
    dot_general x6 -> x4, matrix products: 35 us -> 15.5 us  [dot_t(): lax.dot_general(a, b, (((1,), (1,)), ((), ())), preferred_element_type=f32)]
    broadcast_in_dim x10 -> x3, local copies, waits for them, and re-layouts: 17.3 us -> 0.02 us  [the longest x1 0.01 us: shards(): wx, wdt, bdt, wout = (own(w_x), own(w_dt), own(b_dt)[None], own(w_out))]
    dot_general x9 -> x10, matrix products: 33.9 us -> 18.2 us  [contract_rows(): lax.dot_general(left, right, (((0,), (0,)), ((), ())), preferred_element_...]
    all_to_all x0 -> x1, blocking collectives: none -> 8.91 us  [across_seq(): lax.all_to_all(blocks, 'seq', split_axis=0, concat_axis=0, tiled=True)]
    dot_general x9 -> x7, matrix products: 30 us -> 23.8 us  [dot(): lax.dot_general(a, b, (((1,), (0,)), ((), ())), preferred_element_type=f32)]
    unnamed x124 -> x148, local copies, waits for them, and re-layouts: 16 us -> 20.4 us
  transfers between devices with their start and end apart: 26 -> 30, of which waited for: 13 -> 14; matrix products, arithmetic and copies ran while one was open for 21% -> 16% of each run, Pallas kernels for 0% -> 31%
where the time goes in v2:
time: 491 us; the launch traced here: 485 us
  Pallas kernels  155 us (32%)
  waiting for transfers between devices  130 us (26%)
  matrix products  57.5 us (12%)
  other arithmetic  49.4 us (10%)
  local copies, waits for them, and re-layouts  41 us (8%)
  starting transfers between devices  26.5 us (5%)
  between operations  16.4 us (3%)
  blocking collectives  8.91 us (2%)
    ppermute x26, waiting for transfers between devices, partner(): lax.ppermute(block, axis, [(i, i ^ bit) for i in range(lax.axis_size(axis...  103 us
    pallas_call x2, Pallas kernels, scan_adjoint(): pl.pallas_call(adjoint_kernel, grid=(blocks,), in_specs=[narrow, wide, wi...  90.7 us
    pallas_call x2, Pallas kernels, scan_forward(): pl.pallas_call(scan_kernel, grid=(blocks,), in_specs=[pl.BlockSpec((TB, p...  45.8 us
    dot_general x7, matrix products, dot(): lax.dot_general(a, b, (((1,), (0,)), ((), ())), preferred_element_type=f32)  23.8 us
    all_gather x1, waiting for transfers between devices, shards(): lax.all_gather(jnp.concatenate([early[:rows_each], mine], axis=0), 'dp',...  22.2 us
    unnamed x148, local copies, waits for them, and re-layouts  20.4 us
    ppermute x26, starting transfers between devices, partner(): lax.ppermute(block, axis, [(i, i ^ bit) for i in range(lax.axis_size(axis...  18.5 us
    dot_general x10, matrix products, contract_rows(): lax.dot_general(left, right, (((0,), (0,)), ((), ())), preferred_element_...  18.2 us
  transfers between devices with their start and end apart: 30, of which 14 were waited for; matrix products, arithmetic and copies ran while one was open for 16% of the time, Pallas kernels for 31%

profile of v2, /device:TPU:0, one launch (start us, length us, event | category | flops | bytes accessed | tf_op | source)
XLA Modules:
  0.0 485.0 jit_solution(17005848130992227155)
XLA Ops:
  11.0 1.5 fusion.47
  12.5 3.0 collective-permute-start
  15.5 17.6 %collective-permute-done = bf16[1,1,256,1536]{3,2,1,0:T(8,128)(2,1)} collective-permute-done((bf16[1,1,256,1536]{3,2,1,0:T(8,128)(2,1)S(1)}, bf16[1,1,256,1536]{3,2,1,0:T(8,128)(2,1)}, u32[]{:S(2)}, u32[]{:S(2)}) %collective-permute-start) | collective-permute-done | bytes 786464 | tf_op jit(solution)/shard_map/ppermute | solution.py:310
  33.2 1.7 broadcast_select_fusion.9
  38.0 2.0 collective-permute-done.1
  40.0 1.6 broadcast_select_fusion.3
  41.9 1.7 copy-done.35
  43.6 4.3 fusion.26
  48.2 3.4 multiply_convert_fusion.2
  56.4 1.8 collective-permute-start.3
  61.8 3.0 collective-permute-done.3
  64.9 2.0 fusion.29.u_ref
  67.0 1.8 collective-permute-start.5
  68.8 22.8 %scan_out.2 = (f32[1024,768]{1,0:T(8,128)S(1)}, bf16[8,2064,768]{2,1,0:T(8,128)(2,1)}, f32[1024,768]{1,0:T(8,128)S(1)}) custom-call(bf16[1024,128]{1,0:T(8,128)(2,1)S(1)} %pad_maximum_fusion.13.p_ref, bf16[1024,768]{1,0:T(8,128)(2,1)S(1)} %get-tuple-element.98.u_ref, bf16[768,128]{1,0:T(8,128)(2,1)S(1)} %pad.10.wdt_ref, ...), custom_call_target="tpu_custom_call" | custom-call | flops 25165824000 | bytes 62914560 | tf_op jit(solution)/shard_map/scan_out/pallas_call | solution.py:119
  91.6 1.6 copy-done.20
  94.7 23.0 %scan_out.3 = (bf16[1024,768]{1,0:T(8,128)(2,1)S(1)}, bf16[8,2064,768]{2,1,0:T(8,128)(2,1)}, f32[1024,768]{1,0:T(8,128)S(1)}) custom-call(bf16[1024,128]{1,0:T(8,128)(2,1)S(1)} %fusion.60.p_ref, bf16[1024,768]{1,0:T(8,128)(2,1)S(1)} %fusion.29.u_ref, bf16[768,128]{1,0:T(8,128)(2,1)S(1)} %pad.10.wdt_ref, f32[1,768]{1,0:T(1,128)S(1)} %broadcast_in_dim.26.bdt_ref, ...), custom_call_target="tpu_custom_call" | custom-call | flops 25165824000 | bytes 62914560 | tf_op jit(solution)/shard_map/scan_out/pallas_call | solution.py:119
  118.0 1.5 copy-done.21
  119.8 4.3 fusion.16
  124.1 2.4 fusion.6
  126.6 7.6 %fusion.7 = (bf16[768]{0:T(1024)(128)(2,1)}, f32[1024,768]{1,0:T(8,128)}, bf16[1024,768]{1,0:T(8,128)(2,1)S(1)}, bf16[1024,768]{1,0:T(8,128)(2,1)S(1)}) fusion(bf16[1024,768]{1,0:T(8,128)(2,1)S(1)} %get-tuple-element.98.u_ref, f32[1024,768]{1,0:T(8,128)S(1)} %fusion.16, f32[1024,768]{1,0:T(8,128)S(1)} %fusion.6, bf16[1024,1536]{1,0:T(8,128)(2,1)S(1)} %bitcast.148, ...), kind=kOutput, calls=%fused_computation.14 | convolution fusion | flops 2429287680 | bytes 19662340 | tf_op jit(solution)/shard_map/dot_general | solution.py:18
  137.1 2.9 convolution_convert_fusion.1
  140.3 2.4 pad_maximum_fusion
  143.1 3.9 fusion.30.g_ref
  147.1 44.2 %scan_back.2 = (f32[1024,768]{1,0:T(8,128)S(1)}, f32[1024,128]{1,0:T(8,128)S(1)}, f32[768,128]{1,0:T(8,128)S(1)}, f32[1,768]{1,0:T(1,128)S(1)}, f32[16,768]{1,0:T(8,128)S(1)}) custom-call(bf16[1024,128]{1,0:T(8,128)(2,1)S(1)} %pad_maximum_fusion.13.p_ref, f32[1024,768]{1,0:T(8,128)} %copy-done.20, bf16[1024,768]{1,0:T(8,128)(2,1)S(1)} %get-tuple-element.98.u_ref, ...), custom_call_target="tpu_custom_call" | custom-call | flops 50331648000 | bytes 125829120 | tf_op jit(solution)/shard_map/scan_back/pallas_call | solution.py:254
  192.6 1.7 copy-done.13
  195.9 46.5 %scan_back.3 = (bf16[1024,768]{1,0:T(8,128)(2,1)S(1)}, f32[1024,128]{1,0:T(8,128)S(1)}, f32[768,128]{1,0:T(8,128)S(1)}, f32[1,768]{1,0:T(1,128)S(1)}, f32[16,768]{1,0:T(8,128)S(1)}) custom-call(bf16[1024,128]{1,0:T(8,128)(2,1)S(1)} %copy-done.16, f32[1024,768]{1,0:T(8,128)} %copy-done.21, bf16[1024,768]{1,0:T(8,128)(2,1)S(1)} %copy-done.19, ...), custom_call_target="tpu_custom_call" | custom-call | flops 50331648000 | bytes 125829120 | tf_op jit(solution)/shard_map/scan_back/pallas_call | solution.py:254
  246.0 8.9 %all_to_all.15 = bf16[4,48,768]{2,1,0:T(8,128)(2,1)S(1)} all-to-all(bf16[4,48,768]{2,1,0:T(8,128)(2,1)S(1)} %bitcast.170), channel_id=1, replica_groups=mesh['dp'=8,'seq'=4] {'seq'}, dimensions={0} | all-to-all | bytes 589824 | tf_op jit(solution)/shard_map/all_to_all | solution.py:386
  255.7 4.7 convolution_convert_fusion
  264.2 2.3 collective-permute-done.9
  268.2 3.9 fusion.1
  272.1 9.6 %collective-permute-done.10 = f32[1024,128]{1,0:T(8,128)S(1)} collective-permute-done((f32[1024,128]{1,0:T(8,128)S(1)}, f32[1024,128]{1,0:T(8,128)S(1)}, u32[]{:S(2)}, u32[]{:S(2)}) %collective-permute-start.10) | collective-permute-done | bytes 524320 | tf_op jit(solution)/shard_map/ppermute | solution.py:310
  281.8 3.7 convert_add_fusion.1
  287.1 1.8 multiply_multiply_fusion
  289.0 3.0 multiply_reduce_fusion
  292.0 4.6 fusion.22
  296.6 4.8 add_convert_fusion
  303.1 1.9 copy-done.37
  305.0 1.8 convolution_convert_fusion.3
  308.1 1.8 convolution_convert_fusion.2
  314.0 22.2 %all-gather.3.cloned.1.call-done = bf16[3072,768]{1,0:T(8,128)(2,1)} async-done(((bf16[384,768]{1,0:T(8,128)(2,1)}), bf16[3072,768]{1,0:T(8,128)(2,1)}) %all-gather.3.cloned.1.call-update) | async-done | bytes 4718608 | tf_op jit(solution)/shard_map/all_gather | solution.py:566
  337.6 2.2 constant_dynamic-slice_fusion.1
  340.3 2.3 convert_add_fusion
  342.7 1.6 copy-done.26
  346.7 2.4 dynamic-slice_convert_fusion.1
  349.7 6.1 %join_out.1 = f32[768,1536]{1,0:T(8,128)} custom-call(bf16[8,384,768]{2,1,0:T(8,128)(2,1)} %bitcast.136), custom_call_target="tpu_custom_call" | custom-call | bytes 25165824 | tf_op jit(solution)/shard_map/join_out/pallas_call | solution.py:401
  355.8 6.1 %join_gate.1._ = f32[384,6144]{1,0:T(8,128)} custom-call(bf16[8,384,768]{2,1,0:T(8,128)(2,1)} %bitcast.137), custom_call_target="tpu_custom_call" | custom-call | bytes 25165824 | tf_op jit(solution)/shard_map/join_gate/pallas_call | solution.py:423
  363.4 1.6 convert_add_fusion.4
  365.0 1.6 collective-permute-start.16
  367.2 1.5 collective-permute-start.21
  368.7 8.6 %collective-permute-done.16 = bf16[2,1,1,192,384]{4,3,2,1,0:T(8,128)(2,1)S(1)} collective-permute-done((bf16[2,1,1,192,384]{4,3,2,1,0:T(8,128)(2,1)S(1)}, bf16[2,1,1,192,384]{4,3,2,1,0:T(8,128)(2,1)S(1)}, u32[]{:S(2)}, u32[]{:S(2)}) %collective-permute-start.16) | collective-permute-done | bytes 294944 | tf_op jit(solution)/shard_map/ppermute | solution.py:310
  377.5 16.0 %collective-permute-done.17 = bf16[1,1,1,192,384]{4,3,2,1,0:T(8,128)(2,1)S(1)} collective-permute-done((bf16[1,1,1,192,384]{4,3,2,1,0:T(8,128)(2,1)S(1)}, bf16[1,1,1,192,384]{4,3,2,1,0:T(8,128)(2,1)S(1)}, u32[]{:S(2)}, u32[]{:S(2)}) %collective-permute-start.17) | collective-permute-done | bytes 147488 | tf_op jit(solution)/shard_map/ppermute | solution.py:310
  394.2 3.9 all-to-all-start.1
  399.6 1.5 collective-permute-start.22
  401.2 2.0 fusion.34
  403.3 4.3 collective-permute-done.22
  409.2 3.6 all-to-all-start.2
  412.9 4.7 all-to-all-done.2
  417.6 1.5 collective-permute-start.23
  420.3 4.1 collective-permute-done.23
  424.7 6.2 %collective-permute-done.19 = bf16[2,1,1,192,384]{4,3,2,1,0:T(8,128)(2,1)S(1)} collective-permute-done((bf16[2,1,1,192,384]{4,3,2,1,0:T(8,128)(2,1)S(1)}, bf16[2,1,1,192,384]{4,3,2,1,0:T(8,128)(2,1)S(1)}, u32[]{:S(2)}, u32[]{:S(2)}) %collective-permute-start.19) | collective-permute-done | bytes 294944 | tf_op jit(solution)/shard_map/ppermute | solution.py:310
  431.1 14.5 %collective-permute-done.24 = bf16[1,1,2,288,384]{4,3,2,1,0:T(8,128)(2,1)S(1)} collective-permute-done((bf16[1,1,2,288,384]{4,3,2,1,0:T(8,128)(2,1)S(1)}, bf16[1,1,2,288,384]{4,3,2,1,0:T(8,128)(2,1)S(1)}, u32[]{:S(2)}, u32[]{:S(2)}) %collective-permute-start.24) | collective-permute-done | bytes 442400 | tf_op jit(solution)/shard_map/ppermute | solution.py:310
  446.0 3.5 convert_add_fusion.3
  450.8 15.1 %collective-permute-done.25 = bf16[2,1,2,288,384]{4,3,2,1,0:T(8,128)(2,1)S(1)} collective-permute-done((bf16[2,1,2,288,384]{4,3,2,1,0:T(8,128)(2,1)S(1)}, bf16[2,1,2,288,384]{4,3,2,1,0:T(8,128)(2,1)S(1)}, u32[]{:S(2)}, u32[]{:S(2)}) %collective-permute-start.25) | collective-permute-done | bytes 884768 | tf_op jit(solution)/shard_map/ppermute | solution.py:310
  471.5 6.4 %join_in.1 = f32[384,6144]{1,0:T(8,128)} custom-call(bf16[8,192,384]{2,1,0:T(8,128)(2,1)} %bitcast.146, bf16[8,288,384]{2,1,0:T(8,128)(2,1)} %bitcast.139, f32[384,6144]{1,0:T(8,128)} %join_gate.1._), custom_call_target="tpu_custom_call", output_to_operand_aliasing={{}: (2, {})} | custom-call | bytes 25165824 | tf_op jit(solution)/shard_map/join_in/pallas_call | solution.py:449
  (275 shorter events, 61.9 us)
Async XLA Ops:
  7.2 44.4 %copy-start = (bf16[3072,128]{1,0:T(8,128)(2,1)S(1)}, bf16[3072,128]{1,0:T(8,128)(2,1)}, u32[]{:S(2)}) copy-start(bf16[3072,128]{1,0:T(8,128)(2,1)} %param.17) | copy-start | bytes 2359300
  7.2 26.0 %copy-start.24 = (bf16[1,256,1536]{2,1,0:T(8,128)(2,1)S(1)}, bf16[1,256,1536]{2,1,0:T(8,128)(2,1)}, u32[]{:S(2)}) copy-start(bf16[1,256,1536]{2,1,0:T(8,128)(2,1)} %param.13) | copy-start | bytes 2359300
  7.2 237.7 %reduce-scatter.2.cloned.1.call-start = ((), (), s32[]{:S(2)}) async-start(), calls=%async_computation.4 | async-start | bytes 5308416 | tf_op jit(solution)/shard_map/reduce_scatter | solution.py:554
  8.1 26.8 %copy-start.45 = (f32[1536]{0:T(1024)}, f32[1536]{0:T(1024)S(1)}, u32[]{:S(2)}) copy-start(f32[1536]{0:T(1024)S(1)} %get-tuple-element.95) | copy-start | bytes 18436
  8.1 44.3 %copy-start.47 = (f32[1536]{0:T(1024)}, f32[1536]{0:T(1024)S(1)}, u32[]{:S(2)}) copy-start(f32[1536]{0:T(1024)S(1)} %get-tuple-element.93) | copy-start | bytes 18436
  9.5 25.4 %copy-start.49 = (f32[256]{0:T(256)}, f32[256]{0:T(256)S(1)}, u32[]{:S(2)}) copy-start(f32[256]{0:T(256)S(1)} %broadcast_multiply_fusion) | copy-start | bytes 3076
  11.0 23.9 %copy-start.61 = (f32[256]{0:T(256)}, f32[256]{0:T(256)S(1)}, u32[]{:S(2)}) copy-start(f32[256]{0:T(256)S(1)} %fusion.39) | copy-start | bytes 3076
  11.0 23.9 %copy-start.59 = (f32[256]{0:T(256)}, f32[256]{0:T(256)S(1)}, u32[]{:S(2)}) copy-start(f32[256]{0:T(256)S(1)} %fusion.91) | copy-start | bytes 3076
  12.5 20.7 %collective-permute-start = (bf16[1,1,256,1536]{3,2,1,0:T(8,128)(2,1)S(1)}, bf16[1,1,256,1536]{3,2,1,0:T(8,128)(2,1)}, u32[]{:S(2)}, u32[]{:S(2)}) collective-permute-start(bf16[1,1,256,1536]{3,2,1,0:T(8,128)(2,1)S(1)} %fusion.47), channel_id=1, source_target_pairs={{0,2},{1,3},{2,0},{3,1},{4,6},{5,7},{6,4},{7,5},{8,10},{9,11},{10,... | collective-permute-start | bytes 2359304 | tf_op jit(solution)/shard_map/ppermute | solution.py:310
  36.2 3.8 collective-permute-start.1
  37.9 10.2 %copy-start.51 = (f32[768]{0:T(1024)}, f32[768]{0:T(1024)S(1)}, u32[]{:S(2)}) copy-start(f32[768]{0:T(1024)S(1)} %get-tuple-element.89) | copy-start | bytes 9220
  37.9 10.2 %copy-start.53 = (f32[768]{0:T(1024)}, f32[768]{0:T(1024)S(1)}, u32[]{:S(2)}) copy-start(f32[768]{0:T(1024)S(1)} %get-tuple-element.90) | copy-start | bytes 9220
  38.0 10.2 %copy-start.55 = (f32[768]{0:T(1024)}, f32[768]{0:T(1024)S(1)}, u32[]{:S(2)}) copy-start(f32[768]{0:T(1024)S(1)} %get-tuple-element.91) | copy-start | bytes 9220
  38.0 10.2 %copy-start.57 = (f32[768]{0:T(1024)}, f32[768]{0:T(1024)S(1)}, u32[]{:S(2)}) copy-start(f32[768]{0:T(1024)S(1)} %get-tuple-element.92) | copy-start | bytes 9220
  52.2 3.1 collective-permute-start.2
  56.4 8.4 %collective-permute-start.3 = (f32[512,128]{1,0:T(8,128)S(1)}, f32[512,128]{1,0:T(8,128)S(1)}, u32[]{:S(2)}, u32[]{:S(2)}) collective-permute-start(f32[512,128]{1,0:T(8,128)S(1)} %bitcast_add_fusion), channel_id=1, source_target_pairs={{0,2},{1,3},{2,0},{3,1},{4,6},{5,7},{6,4},{7,5},{8,10},{9,11},{10,... | collective-permute-start | bytes 786440 | tf_op jit(solution)/shard_map/ppermute | solution.py:310
  58.3 84.8 %copy-start.65 = (s32[1024]{0:T(1024)}, s32[1024]{0:T(1024)S(1)}, u32[]{:S(2)}) copy-start(s32[1024]{0:T(1024)S(1)} %fusion.83) | copy-start | bytes 12292
  60.0 64.1 %copy-start.63 = (f32[768]{0:T(1024)}, f32[768]{0:T(1024)S(1)}, u32[]{:S(2)}) copy-start(f32[768]{0:T(1024)S(1)} %dynamic_slice.114) | copy-start | bytes 9220
  60.1 86.9 %copy-start.5 = (bf16[768,128]{1,0:T(8,128)(2,1)}, bf16[768,128]{1,0:T(8,128)(2,1)S(1)}, u32[]{:S(2)}) copy-start(bf16[768,128]{1,0:T(8,128)(2,1)S(1)} %pad.10.wdt_ref) | copy-start | bytes 589828
  61.0 86.0 %copy-start.7 = (bf16[16,768]{1,0:T(8,128)(2,1)}, bf16[16,768]{1,0:T(8,128)(2,1)S(1)}, u32[]{:S(2)}) copy-start(bf16[16,768]{1,0:T(8,128)(2,1)S(1)} %bitcast_convert_fusion.1.alow_ref) | copy-start | bytes 73732
  64.8 2.1 collective-permute-start.4
  66.9 27.7 %copy-start.18 = (bf16[1024,768]{1,0:T(8,128)(2,1)}, bf16[1024,768]{1,0:T(8,128)(2,1)S(1)}, u32[]{:S(2)}) copy-start(bf16[1024,768]{1,0:T(8,128)(2,1)S(1)} %fusion.29.u_ref) | copy-start | bytes 4718596
  67.0 27.0 %collective-permute-start.5 = (bf16[1,1,256,1536]{3,2,1,0:T(8,128)(2,1)S(1)}, bf16[1,1,256,1536]{3,2,1,0:T(8,128)(2,1)S(1)}, u32[]{:S(2)}, u32[]{:S(2)}) collective-permute-start(bf16[1,1,256,1536]{3,2,1,0:T(8,128)(2,1)S(1)} %bitcast.159), channel_id=1, source_target_pairs={{0,2},{1,3},{2,0},{3,1},{4,6},{5,7},{6,4},{7,5},{8,10},{9,11},{10,... | collective-permute-start | bytes 2359304 | tf_op jit(solution)/shard_map/ppermute | solution.py:310
  94.3 23.4 %collective-permute-start.6 = (bf16[2,1,256,1536]{3,2,1,0:T(8,128)(2,1)S(1)}, bf16[2,1,256,1536]{3,2,1,0:T(8,128)(2,1)S(1)}, u32[]{:S(2)}, u32[]{:S(2)}) collective-permute-start(bf16[2,1,256,1536]{3,2,1,0:T(8,128)(2,1)S(1)} %pad_maximum_fusion.6), channel_id=1, source_target_pairs={{0,1},{1,0},{2,3},{3,2},{4,5},{5,4},{6,7},{7,6},{8,9},{9,8},{10,11... | collective-permute-start | bytes 4718600 | tf_op jit(solution)/shard_map/ppermute | solution.py:310
  142.7 193.5 %all-gather.3.cloned.1.call-start = ((), (), s32[]{:S(2)}) async-start(), calls=%async_computation.5 | async-start | bytes 5308416 | tf_op jit(solution)/shard_map/all_gather | solution.py:566
  147.0 47.2 %copy-start.16 = (bf16[1024,128]{1,0:T(8,128)(2,1)S(1)}, bf16[1024,128]{1,0:T(8,128)(2,1)}, u32[]{:S(2)}) copy-start(bf16[1024,128]{1,0:T(8,128)(2,1)} %copy-done.15) | copy-start | bytes 786436
  147.0 47.2 %copy-start.19 = (bf16[1024,768]{1,0:T(8,128)(2,1)S(1)}, bf16[1024,768]{1,0:T(8,128)(2,1)}, u32[]{:S(2)}) copy-start(bf16[1024,768]{1,0:T(8,128)(2,1)} %copy-done.18) | copy-start | bytes 4718596
  261.9 6.2 %copy-start.10 = (f32[1,768]{1,0:T(1,128)S(1)}, f32[1,768]{1,0:T(1,128)}, u32[]{:S(2)}) copy-start(f32[1,768]{1,0:T(1,128)} %copy-done.9) | copy-start | bytes 9220
  261.9 6.2 %copy-start.12 = (f32[1,768]{1,0:T(1,128)S(1)}, f32[1,768]{1,0:T(1,128)}, u32[]{:S(2)}) copy-start(f32[1,768]{1,0:T(1,128)} %copy-done.11) | copy-start | bytes 9220
  261.9 6.2 %copy-start.67 = (bf16[768]{0:T(1024)(128)(2,1)S(1)}, bf16[768]{0:T(1024)(128)(2,1)}, u32[]{:S(2)}) copy-start(bf16[768]{0:T(1024)(128)(2,1)} %get-tuple-element.96) | copy-start | bytes 4612
  261.9 6.2 %copy-start.66 = (s32[1024]{0:T(1024)S(1)}, s32[1024]{0:T(1024)}, u32[]{:S(2)}) copy-start(s32[1024]{0:T(1024)} %copy-done.65) | copy-start | bytes 12292
  261.9 19.9 %collective-permute-start.7 = (bf16[2,1,256,1536]{3,2,1,0:T(8,128)(2,1)}, bf16[2,1,256,1536]{3,2,1,0:T(8,128)(2,1)}, u32[]{:S(2)}, u32[]{:S(2)}) collective-permute-start(bf16[2,1,256,1536]{3,2,1,0:T(8,128)(2,1)} %constant_dynamic-slice_fusion.4), channel_id=1, source_target_pairs={{0,1},{1,0},{2,3},{3,2},{4,5},{5,4},{6,7},{7,6},{8,9},{9,8},{10,11... | collective-permute-start | bytes 4718600 | tf_op jit(solution)/shard_map/ppermute | solution.py:310
  262.9 3.6 collective-permute-start.9
  267.6 14.0 %collective-permute-start.10 = (f32[1024,128]{1,0:T(8,128)S(1)}, f32[1024,128]{1,0:T(8,128)S(1)}, u32[]{:S(2)}, u32[]{:S(2)}) collective-permute-start(f32[1024,128]{1,0:T(8,128)S(1)} %select_add_fusion), channel_id=1, source_target_pairs={{0,2},{1,3},{2,0},{3,1},{4,6},{5,7},{6,4},{7,5},{8,10},{9,11},{10,... | collective-permute-start | bytes 1572872 | tf_op jit(solution)/shard_map/ppermute | solution.py:310
  268.2 13.6 %copy-start.39 = (bf16[1024,1536]{1,0:T(8,128)(2,1)S(1)}, bf16[1024,1536]{1,0:T(8,128)(2,1)}, u32[]{:S(2)}) copy-start(bf16[1024,1536]{1,0:T(8,128)(2,1)} %copy-done.38) | copy-start | bytes 9437188
  281.6 5.4 %copy-start.68 = (f32[1024,768]{1,0:T(8,128)S(1)}, f32[1024,768]{1,0:T(8,128)}, u32[]{:S(2)}) copy-start(f32[1024,768]{1,0:T(8,128)} %get-tuple-element.53.g_ref) | copy-start | bytes 9437188
  281.7 3.9 collective-permute-start.11
  281.8 5.2 %copy-start.42 = (f32[1024,768]{1,0:T(8,128)S(1)}, f32[1024,768]{1,0:T(8,128)}, u32[]{:S(2)}) copy-start(f32[1024,768]{1,0:T(8,128)} %get-tuple-element.99) | copy-start | bytes 9437188
  301.4 5.5 %copy-start.40 = (bf16[1024,1536]{1,0:T(8,128)(2,1)}, bf16[1024,1536]{1,0:T(8,128)(2,1)S(1)}, u32[]{:S(2)}) copy-start(bf16[1024,1536]{1,0:T(8,128)(2,1)S(1)} %add_convert_fusion) | copy-start | bytes 9437188
  302.7 37.6 %collective-permute-start.12 = (bf16[2,1,256,1536]{3,2,1,0:T(8,128)(2,1)}, bf16[2,1,256,1536]{3,2,1,0:T(8,128)(2,1)}, u32[]{:S(2)}, u32[]{:S(2)}) collective-permute-start(bf16[2,1,256,1536]{3,2,1,0:T(8,128)(2,1)} %constant_dynamic-slice_fusion.3), channel_id=1, source_target_pairs={{0,1},{1,0},{2,3},{3,2},{4,5},{5,4},{6,7},{7,6},{8,9},{9,8},{10,11... | collective-permute-start | bytes 4718600 | tf_op jit(solution)/shard_map/ppermute | solution.py:310
  312.1 24.0 %copy-start.33 = (bf16[4,8,48,384]{3,2,0,1:T(8,128)(2,1)S(1)}, bf16[4,8,48,384]{3,2,0,1:T(8,128)(2,1)}, u32[]{:S(2)}) copy-start(bf16[4,8,48,384]{3,2,0,1:T(8,128)(2,1)} %copy.34) | copy-start | bytes 3538948
  337.0 24.9 %collective-permute-start.14 = (bf16[2,2,1,192,384]{4,3,2,1,0:T(8,128)(2,1)}, bf16[2,2,1,192,384]{4,3,2,1,0:T(8,128)(2,1)S(1)}, u32[]{:S(2)}, u32[]{:S(2)}) collective-permute-start(bf16[2,2,1,192,384]{4,3,2,1,0:T(8,128)(2,1)} %constant_dynamic-slice_fusion.2), channel_id=1, source_target_pairs={{0,4},{4,0},{8,12},{12,8},{16,20},{20,16},{24,28},{28,24},{1,5},{5... | collective-permute-start | bytes 1769480 | tf_op jit(solution)/shard_map/ppermute | solution.py:310
  339.8 22.3 %collective-permute-start.15 = (bf16[2,1,2,288,384]{4,3,2,1,0:T(8,128)(2,1)}, bf16[2,1,2,288,384]{4,3,2,1,0:T(8,128)(2,1)}, u32[]{:S(2)}, u32[]{:S(2)}) collective-permute-start(bf16[2,1,2,288,384]{4,3,2,1,0:T(8,128)(2,1)} %constant_dynamic-slice_fusion.1), channel_id=1, source_target_pairs={{0,8},{4,12},{8,0},{12,4},{16,24},{20,28},{24,16},{28,20},{1,9},{5... | collective-permute-start | bytes 2654216 | tf_op jit(solution)/shard_map/ppermute | solution.py:310
  345.3 21.3 %collective-permute-start.13 = (bf16[1,1,256,1536]{3,2,1,0:T(8,128)(2,1)}, bf16[1,1,256,1536]{3,2,1,0:T(8,128)(2,1)S(1)}, u32[]{:S(2)}, u32[]{:S(2)}) collective-permute-start(bf16[1,1,256,1536]{3,2,1,0:T(8,128)(2,1)} %dynamic-slice_convert_fusion), channel_id=1, source_target_pairs={{0,2},{1,3},{2,0},{3,1},{4,6},{5,7},{6,4},{7,5},{8,10},{9,11},{10,... | collective-permute-start | bytes 2359304 | tf_op jit(solution)/shard_map/ppermute | solution.py:310
  349.1 96.8 %collective-permute-start.8 = (bf16[1,1,256,1536]{3,2,1,0:T(8,128)(2,1)}, bf16[1,1,256,1536]{3,2,1,0:T(8,128)(2,1)}, u32[]{:S(2)}, u32[]{:S(2)}) collective-permute-start(bf16[1,1,256,1536]{3,2,1,0:T(8,128)(2,1)} %dynamic-slice_convert_fusion.1), channel_id=1, source_target_pairs={{0,2},{1,3},{2,0},{3,1},{4,6},{5,7},{6,4},{7,5},{8,10},{9,11},{10,... | collective-permute-start | bytes 2359304 | tf_op jit(solution)/shard_map/ppermute | solution.py:310
  365.0 12.4 %copy-start.32 = (f32[2,1,2,288,384]{4,3,2,1,0:T(8,128)}, f32[2,1,2,288,384]{4,3,2,1,0:T(8,128)S(1)}, u32[]{:S(2)}) copy-start(f32[2,1,2,288,384]{4,3,2,1,0:T(8,128)S(1)} %convert_add_fusion.4) | copy-start | bytes 5308420
  365.0 12.5 %copy-start.62 = (f32[256]{0:T(256)S(1)}, f32[256]{0:T(256)}, u32[]{:S(2)}) copy-start(f32[256]{0:T(256)} %copy-done.61) | copy-start | bytes 3076
  365.0 12.3 %collective-permute-start.16 = (bf16[2,1,1,192,384]{4,3,2,1,0:T(8,128)(2,1)S(1)}, bf16[2,1,1,192,384]{4,3,2,1,0:T(8,128)(2,1)S(1)}, u32[]{:S(2)}, u32[]{:S(2)}) collective-permute-start(bf16[2,1,1,192,384]{4,3,2,1,0:T(8,128)(2,1)S(1)} %dynamic-slice_convert_fusion.3), channel_id=1, source_target_pairs={{0,8},{4,12},{8,0},{12,4},{16,24},{20,28},{24,16},{28,20},{1,9},{5... | collective-permute-start | bytes 884744 | tf_op jit(solution)/shard_map/ppermute | solution.py:310
  367.2 34.0 %copy-start.60 = (f32[256]{0:T(256)S(1)}, f32[256]{0:T(256)}, u32[]{:S(2)}) copy-start(f32[256]{0:T(256)} %copy-done.59) | copy-start | bytes 3076
  367.2 31.0 %collective-permute-start.21 = (bf16[1,1,2,288,384]{4,3,2,1,0:T(8,128)(2,1)S(1)}, bf16[1,1,2,288,384]{4,3,2,1,0:T(8,128)(2,1)}, u32[]{:S(2)}, u32[]{:S(2)}) collective-permute-start(bf16[1,1,2,288,384]{4,3,2,1,0:T(8,128)(2,1)S(1)} %dynamic-slice_convert_fusion.2), channel_id=1, source_target_pairs={{0,16},{4,20},{8,24},{12,28},{16,0},{20,4},{24,8},{28,12},{1,17},{... | collective-permute-start | bytes 1327112 | tf_op jit(solution)/shard_map/ppermute | solution.py:310
  377.4 16.1 %collective-permute-start.17 = (bf16[1,1,1,192,384]{4,3,2,1,0:T(8,128)(2,1)S(1)}, bf16[1,1,1,192,384]{4,3,2,1,0:T(8,128)(2,1)S(1)}, u32[]{:S(2)}, u32[]{:S(2)}) collective-permute-start(bf16[1,1,1,192,384]{4,3,2,1,0:T(8,128)(2,1)S(1)} %dynamic-slice_convert_fusion.5), channel_id=1, source_target_pairs={{0,16},{4,20},{8,24},{12,28},{16,0},{20,4},{24,8},{28,12},{1,17},{... | collective-permute-start | bytes 442376 | tf_op jit(solution)/shard_map/ppermute | solution.py:310
  394.2 9.0 %all-to-all-start.1 = ((bf16[4,48,384]{2,1,0:T(8,128)(2,1)}), bf16[4,48,384]{2,1,0:T(8,128)(2,1)}, u32[]{:S(2)}, u32[]{:S(2)}) async-start(bf16[4,48,384]{2,1,0:T(8,128)(2,1)} %bitcast.35), calls=%async_computation.2 | async-start | bytes 294912 | tf_op jit(solution)/shard_map/all_to_all | solution.py:386
  399.6 7.9 %collective-permute-start.22 = (bf16[1,1,1,288,384]{4,3,2,1,0:T(8,128)(2,1)S(1)}, bf16[1,1,1,288,384]{4,3,2,1,0:T(8,128)(2,1)}, u32[]{:S(2)}, u32[]{:S(2)}) collective-permute-start(bf16[1,1,1,288,384]{4,3,2,1,0:T(8,128)(2,1)S(1)} %dynamic-slice_convert_fusion.4), channel_id=1, source_target_pairs={{0,4},{4,0},{8,12},{12,8},{16,20},{20,16},{24,28},{28,24},{1,5},{5... | collective-permute-start | bytes 663560 | tf_op jit(solution)/shard_map/ppermute | solution.py:310
  403.2 15.9 %collective-permute-start.18 = (bf16[1,1,1,192,384]{4,3,2,1,0:T(8,128)(2,1)}, bf16[1,1,1,192,384]{4,3,2,1,0:T(8,128)(2,1)}, u32[]{:S(2)}, u32[]{:S(2)}) collective-permute-start(bf16[1,1,1,192,384]{4,3,2,1,0:T(8,128)(2,1)} %bitcast.36), channel_id=1, source_target_pairs={{0,16},{4,20},{8,24},{12,28},{16,0},{20,4},{24,8},{28,12},{1,17},{... | collective-permute-start | bytes 442376 | tf_op jit(solution)/shard_map/ppermute | solution.py:310
  409.2 8.4 %all-to-all-start.2 = ((bf16[4,48,384]{2,1,0:T(8,128)(2,1)}), bf16[4,48,384]{2,1,0:T(8,128)(2,1)S(1)}, u32[]{:S(2)}, u32[]{:S(2)}) async-start(bf16[4,48,384]{2,1,0:T(8,128)(2,1)} %bitcast.38), calls=%async_computation.3 | async-start | bytes 294912 | tf_op jit(solution)/shard_map/all_to_all | solution.py:386
  417.6 6.8 %collective-permute-start.23 = (bf16[1,1,1,288,384]{4,3,2,1,0:T(8,128)(2,1)S(1)}, bf16[1,1,1,288,384]{4,3,2,1,0:T(8,128)(2,1)S(1)}, u32[]{:S(2)}, u32[]{:S(2)}) collective-permute-start(bf16[1,1,1,288,384]{4,3,2,1,0:T(8,128)(2,1)S(1)} %maximum_bitcast_fusion), channel_id=1, source_target_pairs={{0,4},{4,0},{8,12},{12,8},{16,20},{20,16},{24,28},{28,24},{1,5},{5... | collective-permute-start | bytes 663560 | tf_op jit(solution)/shard_map/ppermute | solution.py:310
  420.2 10.7 %collective-permute-start.19 = (bf16[2,1,1,192,384]{4,3,2,1,0:T(8,128)(2,1)S(1)}, bf16[2,1,1,192,384]{4,3,2,1,0:T(8,128)(2,1)S(1)}, u32[]{:S(2)}, u32[]{:S(2)}) collective-permute-start(bf16[2,1,1,192,384]{4,3,2,1,0:T(8,128)(2,1)S(1)} %pad_maximum_fusion.12), channel_id=1, source_target_pairs={{0,8},{4,12},{8,0},{12,4},{16,24},{20,28},{24,16},{28,20},{1,9},{5... | collective-permute-start | bytes 884744 | tf_op jit(solution)/shard_map/ppermute | solution.py:310
  424.4 21.5 %copy-start.44 = (bf16[1,256,1536]{2,1,0:T(8,128)(2,1)S(1)}, bf16[1,256,1536]{2,1,0:T(8,128)(2,1)}, u32[]{:S(2)}) copy-start(bf16[1,256,1536]{2,1,0:T(8,128)(2,1)} %param.25) | copy-start | bytes 2359300
  424.5 21.4 %copy-start.29 = (f32[2,1,256,1536]{3,2,1,0:T(8,128)S(1)}, f32[2,1,256,1536]{3,2,1,0:T(8,128)}, u32[]{:S(2)}) copy-start(f32[2,1,256,1536]{3,2,1,0:T(8,128)} %convert_add_fusion.1) | copy-start | bytes 9437188
  424.6 21.0 %collective-permute-start.24 = (bf16[1,1,2,288,384]{4,3,2,1,0:T(8,128)(2,1)S(1)}, bf16[1,1,2,288,384]{4,3,2,1,0:T(8,128)(2,1)S(1)}, u32[]{:S(2)}, u32[]{:S(2)}) collective-permute-start(bf16[1,1,2,288,384]{4,3,2,1,0:T(8,128)(2,1)S(1)} %pad_maximum_fusion.11), channel_id=1, source_target_pairs={{0,16},{4,20},{8,24},{12,28},{16,0},{20,4},{24,8},{28,12},{1,17},{... | collective-permute-start | bytes 1327112 | tf_op jit(solution)/shard_map/ppermute | solution.py:310
  431.0 15.0 %copy-start.28 = (f32[2,1,256,1536]{3,2,1,0:T(8,128)S(1)}, f32[2,1,256,1536]{3,2,1,0:T(8,128)}, u32[]{:S(2)}) copy-start(f32[2,1,256,1536]{3,2,1,0:T(8,128)} %copy-done.26) | copy-start | bytes 9437188
  431.0 15.0 %copy-start.48 = (f32[1536]{0:T(1024)S(1)}, f32[1536]{0:T(1024)}, u32[]{:S(2)}) copy-start(f32[1536]{0:T(1024)} %copy-done.47) | copy-start | bytes 18436
  431.1 18.4 %collective-permute-start.20 = (bf16[2,2,1,192,384]{4,3,2,1,0:T(8,128)(2,1)S(1)}, bf16[2,2,1,192,384]{4,3,2,1,0:T(8,128)(2,1)S(1)}, u32[]{:S(2)}, u32[]{:S(2)}) collective-permute-start(bf16[2,2,1,192,384]{4,3,2,1,0:T(8,128)(2,1)S(1)} %pad_maximum_fusion.10), channel_id=1, source_target_pairs={{0,4},{4,0},{8,12},{12,8},{16,20},{20,16},{24,28},{28,24},{1,5},{5... | collective-permute-start | bytes 1769480 | tf_op jit(solution)/shard_map/ppermute | solution.py:310
  445.9 20.0 %collective-permute-start.25 = (bf16[2,1,2,288,384]{4,3,2,1,0:T(8,128)(2,1)S(1)}, bf16[2,1,2,288,384]{4,3,2,1,0:T(8,128)(2,1)S(1)}, u32[]{:S(2)}, u32[]{:S(2)}) collective-permute-start(bf16[2,1,2,288,384]{4,3,2,1,0:T(8,128)(2,1)S(1)} %pad_maximum_fusion.8), channel_id=1, source_target_pairs={{0,8},{4,12},{8,0},{12,4},{16,24},{20,28},{24,16},{28,20},{1,9},{5... | collective-permute-start | bytes 2654216 | tf_op jit(solution)/shard_map/ppermute | solution.py:310
  (38 other events, 80.9 us)
Sparse Core Ops, SparseCore 0:
  142.8 95.5 reduce-scatter.1
  255.9 80.2 all-gather.2
